TPU v7x, 128 devices: a whole 4x4x4 slice. The times are simulated.
128 devices in a mesh: dp: 32 (over y, x, z_lo), tensor: 4 (over z_hi, core).
Axes of the slice: x: 4, y: 4, z: 4 (z_hi: 2, z_lo: 2; z = z_hi * 2 + z_lo), core: 2. Of those that a mesh axis runs over, the one named last changes fastest.
Arguments:
- inputs: bfloat16 [16384, 2048], P(('dp', 'tensor')), may hold values from -6 to 6
- cotangent: bfloat16 [16384, 2048], P(('dp', 'tensor')), may hold values from -6 to 6
- lengths: int32 [32, 4], P('dp'), may hold values from 1 to 384, as said below
- qkv_weight: float32 [3, 2048, 2048], P(None, 'dp', 'tensor'), may hold values from -0.125 to 0.125
- out_weight: float32 [2048, 2048], P('tensor', 'dp'), may hold values from -0.5 to 0.5
- up_weight: float32 [2048, 8192], P('dp', 'tensor'), may hold values from -0.125 to 0.125
- down_weight: float32 [8192, 2048], P('tensor', 'dp'), may hold values from -0.0625 to 0.0625
- norm_vectors: float32 [13, 2048], P(None, 'dp'), may hold values from -0.8 to 1.4
- qkv_mean: float32 [3, 2048, 2048], P(None, 'dp', 'tensor'), may hold values from -32 to 32
- qkv_square: float32 [3, 2048, 2048], P(None, 'dp', 'tensor'), may hold values from 137.6256 to 557.056
- out_mean: float32 [2048, 2048], P('tensor', 'dp'), may hold values from -16 to 16
- out_square: float32 [2048, 2048], P('tensor', 'dp'), may hold values from 34.4064 to 137.6256
- up_mean: float32 [2048, 8192], P('dp', 'tensor'), may hold values from -24 to 24
- up_square: float32 [2048, 8192], P('dp', 'tensor'), may hold values from 77.0048 to 311.296
- down_mean: float32 [8192, 2048], P('tensor', 'dp'), may hold values from -56 to 56
- down_square: float32 [8192, 2048], P('tensor', 'dp'), may hold values from 360.448 to 1458.176
- vector_mean: float32 [13, 2048], P(None, 'dp'), may hold values from -48 to 48
- vector_square: float32 [13, 2048], P(None, 'dp'), may hold values from 163.84 to 1245.184
Outputs:
- block_out: bfloat16 [16384, 2048], P(('dp', 'tensor'))
- input_grad: float32 [16384, 2048], P(('dp', 'tensor'))
- qkv_updated: float32 [3, 2048, 2048], P(None, 'dp', 'tensor')
- qkv_moment: float32 [3, 2048, 2048], P(None, 'dp', 'tensor')
- qkv_squares: float32 [3, 2048, 2048], P(None, 'dp', 'tensor')
- out_updated: float32 [2048, 2048], P('tensor', 'dp')
- out_moment: float32 [2048, 2048], P('tensor', 'dp')
- out_squares: float32 [2048, 2048], P('tensor', 'dp')
- up_updated: float32 [2048, 8192], P('dp', 'tensor')
- up_moment: float32 [2048, 8192], P('dp', 'tensor')
- up_squares: float32 [2048, 8192], P('dp', 'tensor')
- down_updated: float32 [8192, 2048], P('tensor', 'dp')
- down_moment: float32 [8192, 2048], P('tensor', 'dp')
- down_squares: float32 [8192, 2048], P('tensor', 'dp')
- vector_updated: float32 [13, 2048], P(None, 'dp')
- vector_moment: float32 [13, 2048], P(None, 'dp')
- vector_squares: float32 [13, 2048], P(None, 'dp')
Inputs may be any that keep to these rules, and one draw needn't show every extreme that they name: `lengths`: each row fills the 512 tokens of its group; its second entry is 384 and its first is under 128.
All inputs are finite; a program needn't handle non-finite values.
Results may differ from a plain program's by a relative error of at most 0.012.
Values may be sent and summed in bfloat16 or wider, within the bound.
A program may use at most 256 MiB of HBM per device.

v0:
```python
import math

import jax
import jax.numpy as jnp
from jax import lax
from jax.sharding import PartitionSpec as P

HD = 256
ROT = 64
UPDATE_STEP = 10


norm_eps = 1e-05
beta_first = 0.9
beta_second = 0.95
adam_eps = 1e-08
matrix_rate = 0.02
vector_rate = 0.2
matrix_decay = 0.01
masked_score = -1e30
inv_root_two = 1.0 / math.sqrt(2.0)
inv_root_tau = 1.0 / math.sqrt(2.0 * math.pi)


def in_one_piece(arrays, axis, dim, along):
    both = jnp.concatenate(arrays, axis=along)
    filled, at, finished = (lax.all_gather(both, axis, axis=dim, tiled=True), 0, [])
    for a in arrays:
        finished.append(lax.slice_in_dim(filled, at, at + a.shape[along], axis=along))
        at += a.shape[along]
    return tuple(finished)


def turned_gather(arrays, axis, dims):
    turned = [jnp.moveaxis(a, dim, 0) for a, dim in zip(arrays, dims)]
    widths = [t[0].size for t in turned]
    both = jnp.concatenate([t.reshape(-1, w) for t, w in zip(turned, widths)], axis=1)
    filled = lax.all_gather(both, axis, axis=0, tiled=True)
    parts = jnp.split(filled, [sum(widths[:k]) for k in range(1, len(widths))], axis=1)
    return tuple(
        (
            jnp.moveaxis(b.reshape(-1, *t.shape[1:]), 0, dim)
            for b, t, dim in zip(parts, turned, dims)
        )
    )


def cut_along(array, dim, size):
    dims = array.shape
    parts = array.reshape(*dims[:dim], size, dims[dim] // size, *dims[dim + 1 :])
    return jnp.moveaxis(parts, dim, 0)


def summed_on_arrival(array, axis, dim):
    parts = cut_along(array, dim, lax.axis_size(axis))
    arrived = lax.all_to_all(parts, axis, split_axis=0, concat_axis=0, tiled=True)
    return arrived.astype(jnp.float32).sum(axis=0)


def sent_together(arrays, axis, dim, along):
    both = jnp.concatenate(arrays, axis=along)
    filled, at, finished = (lax.psum_scatter(both, axis, scatter_dimension=dim, tiled=True), 0, [])
    for a in arrays:
        finished.append(lax.slice_in_dim(filled, at, at + a.shape[along], axis=along))
        at += a.shape[along]
    return tuple(finished)


def from_everyone(array, axis):
    size = lax.axis_size(axis)
    return lax.all_to_all(
        jnp.broadcast_to(array[None], (size, *array.shape)), axis, 0, 0, tiled=True
    )


def over_copies(array, axis):
    return from_everyone(array, axis).sum(axis=0)


def rotary_tables(positions):
    half_rot = ROT // 2
    frequency = jnp.exp(jnp.arange(half_rot, dtype=jnp.float32) * (-2.0 * math.log(10000.0) / ROT))
    angles = positions.astype(jnp.float32)[:, None] * frequency[None, :]
    return (jnp.cos(angles), jnp.sin(angles))


def rotate(values_in, cos_table, sin_table):
    half_rot = ROT // 2
    lead_half = values_in[..., :half_rot]
    tail_half = values_in[..., half_rot:ROT]
    cos_part = cos_table[:, None, :]
    sin_part = sin_table[:, None, :]
    return jnp.concatenate(
        [
            lead_half * cos_part - tail_half * sin_part,
            tail_half * cos_part + lead_half * sin_part,
            values_in[..., ROT:],
        ],
        axis=-1,
    )


def segment_layout(seq_lengths, total_rows):
    seq_ends = jnp.cumsum(seq_lengths)
    seq_starts = seq_ends - seq_lengths
    row_index = jnp.arange(total_rows, dtype=jnp.int32)
    segment = jnp.sum((row_index[:, None] >= seq_ends[None, :]).astype(jnp.int32), axis=1)
    chosen = segment[:, None] == jnp.arange(seq_lengths.shape[0], dtype=jnp.int32)[None, :]
    position = row_index - jnp.sum(jnp.where(chosen, seq_starts[None, :], 0), axis=1)
    return (segment, position)


def adamw(weight, gradient, moment, square, step_rate, decay_rate):
    moment_new = beta_first * moment + (1.0 - beta_first) * gradient
    square_new = beta_second * square + (1.0 - beta_second) * gradient * gradient
    first_fix = 1.0 - beta_first**UPDATE_STEP
    second_fix = 1.0 - beta_second**UPDATE_STEP
    direction = moment_new / first_fix / (jnp.sqrt(square_new / second_fix) + adam_eps)
    weight_new = weight - step_rate * (direction + decay_rate * weight)
    return (weight_new, moment_new, square_new)


def local(
    inputs,
    cotangent,
    lengths,
    qkv_weight,
    out_weight,
    up_weight,
    down_weight,
    norm_vectors,
    qkv_mean,
    qkv_square,
    out_mean,
    out_square,
    up_mean,
    up_square,
    down_mean,
    down_square,
    vector_mean,
    vector_square,
):
    tensor_rank = lax.axis_index("tensor")
    tensor_count = lax.axis_size("tensor")
    shard_rows = inputs.shape[0]
    model_width = inputs.shape[1]
    group_rows, group_cot = in_one_piece((inputs, cotangent), "tensor", 0, 1)
    qkv_full, out_full, up_full, down_full, vector_full = turned_gather(
        (
            qkv_weight.astype(jnp.bfloat16),
            out_weight.astype(jnp.bfloat16),
            up_weight.astype(jnp.bfloat16),
            down_weight.astype(jnp.bfloat16),
            norm_vectors.astype(jnp.bfloat16),
        ),
        "dp",
        (1, 1, 0, 1, 1),
    )
    vector_vals = vector_full.astype(jnp.float32)
    head_cols = qkv_full.shape[2]
    hidden_cols = up_full.shape[1]
    local_heads = head_cols // HD
    qkv_bias = lax.dynamic_slice_in_dim(vector_vals[4:7], tensor_rank * head_cols, head_cols, 1)
    up_bias = lax.dynamic_slice_in_dim(
        vector_vals[9:].reshape(-1), tensor_rank * hidden_cols, hidden_cols, 0
    )
    group_float = group_rows.astype(jnp.float32)
    total_rows = group_float.shape[0]
    centred = group_float - jnp.mean(group_float, axis=-1, keepdims=True)
    inv_scale = lax.rsqrt(jnp.mean(centred * centred, axis=-1, keepdims=True) + norm_eps)
    unit_rows = centred * inv_scale
    norm_one = (unit_rows * vector_vals[0] + vector_vals[1]).astype(jnp.bfloat16)
    norm_two = (unit_rows * vector_vals[2] + vector_vals[3]).astype(jnp.bfloat16)
    segment, position = segment_layout(lengths[0], total_rows)
    cos_table, sin_table = rotary_tables(position)
    qkv_pre = (
        jnp.einsum("gd,cdh->cgh", norm_one, qkv_full, preferred_element_type=jnp.float32)
        + qkv_bias[:, None, :]
    )
    query_rows = rotate(
        qkv_pre[0].reshape(total_rows, local_heads, HD), cos_table, sin_table
    ).astype(jnp.bfloat16)
    key_rows = rotate(qkv_pre[1].reshape(total_rows, local_heads, HD), cos_table, sin_table).astype(
        jnp.bfloat16
    )
    value_rows = qkv_pre[2].reshape(total_rows, local_heads, HD).astype(jnp.bfloat16)
    block_len = min(512, total_rows)
    block_count = total_rows // block_len
    score_scale = HD ** (-0.5)
    row_index = jnp.arange(total_rows, dtype=jnp.int32)

    def block_scores():
        allowed = (segment[:, None] == segment[None, :]) & (
            row_index[None, :] <= row_index[:, None]
        )
        scores = (
            jnp.einsum("qhd,khd->hqk", query_rows, key_rows, preferred_element_type=jnp.float32)
            * score_scale
        )
        return (query_rows, jnp.where(allowed[None], scores, masked_score))

    def forward_block(block_id):
        query_block, scores = block_scores()
        top_score = jnp.max(scores, axis=-1, keepdims=True)
        log_total = top_score + jnp.log(
            jnp.sum(jnp.exp(scores - top_score), axis=-1, keepdims=True)
        )
        soft_weights = jnp.exp(scores - log_total)
        weighted = jnp.einsum(
            "hqk,khd->qhd",
            soft_weights.astype(jnp.bfloat16),
            value_rows,
            preferred_element_type=jnp.float32,
        )
        return (weighted, log_total)

    block_ids = jnp.arange(block_count, dtype=jnp.int32)
    weighted, log_totals = lax.map(forward_block, block_ids)
    mixed_heads = weighted.reshape(total_rows, head_cols).astype(jnp.bfloat16)
    hidden = jnp.dot(norm_two, up_full, preferred_element_type=jnp.float32) + up_bias
    activated = jax.nn.gelu(hidden, approximate=False).astype(jnp.bfloat16)
    partial_sum = jnp.dot(mixed_heads, out_full, preferred_element_type=jnp.float32)
    partial_sum = partial_sum + jnp.dot(activated, down_full, preferred_element_type=jnp.float32)
    branch = summed_on_arrival(partial_sum.astype(jnp.bfloat16), "tensor", 0)
    block_out = (inputs.astype(jnp.float32) + branch + vector_vals[7] + vector_vals[8]).astype(
        jnp.bfloat16
    )
    down_grad = jnp.einsum("gf,gd->fd", activated, group_cot, preferred_element_type=jnp.float32)
    out_grad = jnp.einsum("gh,gd->hd", mixed_heads, group_cot, preferred_element_type=jnp.float32)
    act_grad = jnp.einsum("gd,fd->gf", group_cot, down_full, preferred_element_type=jnp.float32)
    slope = (
        0.5 * (1.0 + lax.erf(hidden * inv_root_two))
        + hidden * jnp.exp(-0.5 * hidden * hidden) * inv_root_tau
    )
    hidden_grad = (act_grad * slope).astype(jnp.bfloat16)
    up_grad = jnp.einsum("gd,gf->df", norm_two, hidden_grad, preferred_element_type=jnp.float32)
    norm_two_grad = jnp.einsum(
        "gf,df->gd", hidden_grad, up_full, preferred_element_type=jnp.float32
    )
    mixed_grad = jnp.einsum("gd,hd->gh", group_cot, out_full, preferred_element_type=jnp.float32)
    mixed_grad = mixed_grad.astype(jnp.bfloat16).reshape(total_rows, local_heads, HD)

    def backward_block(carry, block_id):
        key_grad, value_grad = carry
        query_block, scores = block_scores()
        soft_weights = jnp.exp(scores - log_totals[block_id])
        soft_grad = jnp.einsum(
            "qhd,khd->hqk", mixed_grad, value_rows, preferred_element_type=jnp.float32
        )
        inner = jnp.sum(soft_weights * soft_grad, axis=-1, keepdims=True)
        score_grad = (soft_weights * (soft_grad - inner)).astype(jnp.bfloat16)
        query_grad = (
            jnp.einsum("hqk,khd->qhd", score_grad, key_rows, preferred_element_type=jnp.float32)
            * score_scale
        )
        key_grad = (
            key_grad
            + jnp.einsum(
                "hqk,qhd->khd", score_grad, query_block, preferred_element_type=jnp.float32
            )
            * score_scale
        )
        value_grad = value_grad + jnp.einsum(
            "hqk,qhd->khd",
            soft_weights.astype(jnp.bfloat16),
            mixed_grad,
            preferred_element_type=jnp.float32,
        )
        return ((key_grad, value_grad), query_grad)

    zero_heads = jnp.zeros((total_rows, local_heads, HD), jnp.float32)
    (key_grad, value_grad), query_grads = lax.scan(
        backward_block, (zero_heads, zero_heads), block_ids
    )
    query_grad = query_grads.reshape(total_rows, local_heads, HD)
    query_back = rotate(query_grad, cos_table, -sin_table)
    key_back = rotate(key_grad, cos_table, -sin_table)
    qkv_grad = (
        jnp.stack([query_back, key_back, value_grad])
        .reshape(3, total_rows, head_cols)
        .astype(jnp.bfloat16)
    )
    qkv_weight_grad = jnp.einsum(
        "gd,cgh->cdh", norm_one, qkv_grad, preferred_element_type=jnp.float32
    )
    norm_one_grad = jnp.einsum(
        "cgh,cdh->gd", qkv_grad, qkv_full, preferred_element_type=jnp.float32
    )
    unit_local = lax.dynamic_slice_in_dim(unit_rows, tensor_rank * shard_rows, shard_rows, 0)
    scale_local = lax.dynamic_slice_in_dim(inv_scale, tensor_rank * shard_rows, shard_rows, 0)
    unit_terms = norm_one_grad * vector_vals[0] + norm_two_grad * vector_vals[2]
    norm_rows = jnp.stack(
        [
            jnp.sum(norm_one_grad * unit_rows, axis=0),
            jnp.sum(norm_one_grad, axis=0),
            jnp.sum(norm_two_grad * unit_rows, axis=0),
            jnp.sum(norm_two_grad, axis=0),
        ]
    )
    unit_grad = summed_on_arrival(unit_terms.astype(jnp.bfloat16), "tensor", 0)
    input_grad = cotangent.astype(jnp.float32) + scale_local * (
        unit_grad
        - jnp.mean(unit_grad, axis=-1, keepdims=True)
        - unit_local * jnp.mean(unit_grad * unit_local, axis=-1, keepdims=True)
    )
    cot_total = jnp.sum(cotangent.astype(jnp.float32), axis=0)
    zero_index = tensor_rank * 0
    qkv_bias_grad = jnp.sum(qkv_grad.astype(jnp.float32), axis=1)
    qkv_bias_rows = lax.dynamic_update_slice(
        jnp.zeros((3, model_width), jnp.float32),
        qkv_bias_grad,
        (zero_index, tensor_rank * head_cols),
    )
    up_bias_grad = jnp.sum(hidden_grad.astype(jnp.float32), axis=0)
    up_bias_rows = lax.dynamic_update_slice(
        jnp.zeros((hidden_cols * tensor_count,), jnp.float32),
        up_bias_grad,
        (tensor_rank * hidden_cols,),
    ).reshape(-1, model_width)
    vector_grad = jnp.concatenate(
        [norm_rows, qkv_bias_rows, cot_total[None], cot_total[None], up_bias_rows], axis=0
    )
    qkv_sum, out_sum, up_sum, down_sum, vector_part = (
        lax.psum_scatter(qkv_weight_grad, "dp", scatter_dimension=1, tiled=True),
        lax.psum_scatter(out_grad, "dp", scatter_dimension=1, tiled=True),
        lax.psum_scatter(up_grad, "dp", scatter_dimension=0, tiled=True),
        *sent_together((down_grad, vector_grad), "dp", 1, 0),
    )
    vector_sum = over_copies(vector_part, "tensor")
    qkv_new = adamw(qkv_weight, qkv_sum, qkv_mean, qkv_square, matrix_rate, matrix_decay)
    out_new = adamw(out_weight, out_sum, out_mean, out_square, matrix_rate, matrix_decay)
    up_new = adamw(up_weight, up_sum, up_mean, up_square, matrix_rate, matrix_decay)
    down_new = adamw(down_weight, down_sum, down_mean, down_square, matrix_rate, matrix_decay)
    vector_new = adamw(norm_vectors, vector_sum, vector_mean, vector_square, vector_rate, 0.0)
    return (
        block_out,
        input_grad,
        qkv_new[0],
        qkv_new[1],
        qkv_new[2],
        out_new[0],
        out_new[1],
        out_new[2],
        up_new[0],
        up_new[1],
        up_new[2],
        down_new[0],
        down_new[1],
        down_new[2],
        vector_new[0],
        vector_new[1],
        vector_new[2],
    )


def solution(mesh):
    placed = (
        P(("dp", "tensor"), None),
        P(("dp", "tensor"), None),
        P("dp", None),
        P(None, "dp", "tensor"),
        P("tensor", "dp"),
        P("dp", "tensor"),
        P("tensor", "dp"),
        P(None, "dp"),
        P(None, "dp", "tensor"),
        P(None, "dp", "tensor"),
        P("tensor", "dp"),
        P("tensor", "dp"),
        P("dp", "tensor"),
        P("dp", "tensor"),
        P("tensor", "dp"),
        P("tensor", "dp"),
        P(None, "dp"),
        P(None, "dp"),
    )
    return jax.shard_map(
        local,
        mesh=mesh,
        in_specs=placed,
        out_specs=(
            P(("dp", "tensor"), None),
            P(("dp", "tensor"), None),
            P(None, "dp", "tensor"),
            P(None, "dp", "tensor"),
            P(None, "dp", "tensor"),
            P("tensor", "dp"),
            P("tensor", "dp"),
            P("tensor", "dp"),
            P("dp", "tensor"),
            P("dp", "tensor"),
            P("dp", "tensor"),
            P("tensor", "dp"),
            P("tensor", "dp"),
            P("tensor", "dp"),
            P(None, "dp"),
            P(None, "dp"),
            P(None, "dp"),
        ),
        check_vma=False,
    )
```

profile of v0, /device:TPU:0, one launch (start us, length us, event | category | flops | bytes accessed | tf_op | source)
XLA Modules:
  0.0 2324.6 jit_solution(12176880592147210089)
XLA Ops:
  7.3 2.3 pad_maximum_fusion.1
  9.7 0.7 convert_bitcast_fusion.2
  10.5 1.0 convert_bitcast_fusion.1
  11.7 0.9 copy-done.18
  13.1 0.9 fusion.50
  14.0 1.8 fusion.59
  15.8 35.6 %all-gather.5.cloned.1.call-done = bf16[512,4096]{1,0:T(8,128)(2,1)} async-done(((bf16[128,4096]{1,0:T(8,128)(2,1)}), bf16[512,4096]{1,0:T(8,128)(2,1)}) %all-gather.5.cloned.1.call-update) | async-done | bytes 4194320 | tf_op jit(solution)/shard_map/all_gather | solution.py:27
  51.5 1.9 convert_reduce_fusion.2
  53.4 2.3 fusion.10
  55.7 542.0 %all-gather.3.cloned.1.call-done = bf16[2048,6157]{1,0:T(8,128)(2,1)} async-done(((bf16[64,6157]{1,0:T(8,128)(2,1)}), bf16[2048,6157]{1,0:T(8,128)(2,1)}) %all-gather.3.cloned.1.call-update) | async-done | bytes 25219088 | tf_op jit(solution)/shard_map/all_gather | solution.py:38
  597.8 1.1 convert_bitcast_fusion
  598.9 3.1 slice_reduce_fusion.1
  602.4 5.9 split.20
  608.3 8.9 copy.246
  617.3 7.1 add_bitcast_fusion
  624.4 0.9 slice.184
  625.6 1.0 copy.299
  626.6 1.0 copy.296
  628.4 1.2 subtract_convert_fusion.3
  629.7 2.8 fusion.72
  633.4 0.8 copy-done.4
  634.2 3.3 fusion.41
  638.0 3.5 fusion.45
  641.5 0.8 copy-done.15
  642.3 1.3 convolution_convert_fusion
  643.6 2.0 copy.269
  645.7 1.9 multiply_reduce_fusion.1
  648.2 0.9 fusion.38
  650.8 1.7 pad_maximum_fusion.4
  652.9 1.3 copy.265
  654.5 8.7 convolution_bitcast_fusion
  663.1 18.0 copy.272
  682.0 18.9 fusion.13
  701.0 8.1 convert_reduce_fusion.3
  709.1 1.3 copy-done.49
  710.4 8.6 fusion.63
  719.2 0.9 copy-done.12
  720.1 5.7 fusion.62
  725.8 9.7 multiply_reduce_fusion
  735.5 4.2 all-to-all-start.1
  740.0 1.3 convert_reduce_fusion.5
  741.6 12.5 fusion.39
  754.2 37.8 %all-to-all-done.1 = bf16[4,128,2048]{2,1,0:T(8,128)(2,1)S(1)} async-done(((bf16[4,128,2048]{2,1,0:T(8,128)(2,1)}), bf16[4,128,2048]{2,1,0:T(8,128)(2,1)S(1)}, u32[]{:S(2)}, u32[]{:S(2)}) %all-to-all-start.1) | async-done | bytes 2097184 | tf_op jit(solution)/shard_map/all_to_all | solution.py:56
  792.5 1.5 multiply_reduce_fusion.2
  794.0 2.6 convert_reduce_fusion.6
  796.6 38.7 %concatenate.33 = f32[2061,2048]{1,0:T(8,128)} concatenate(f32[2048,2048]{1,0:T(8,128)} %fusion.39, f32[1,2048]{1,0:T(1,128)S(1)} %bitcast.108, f32[1,2048]{1,0:T(1,128)S(1)} %bitcast.109, f32[1,2048]{1,0:T(1,128)S(1)} %bitcast.107, f32[1,2048]{1,0:T(1,128)S(1)} %bitcast.110, f32[3,2048]{1,0:T(4,128)S(1)} %constant_dynamic-update-slice_fusion.2, f32[1,2048]{1,0:T(1,128)S(1)} %bitcast.104, ...), dimensions={0} | concatenate | bytes 33767424 | tf_op jit(solution)/shard_map/concatenate | solution.py:61
  835.3 17.1 copy.290
  852.4 1.6 copy-done.48
  854.0 7.0 fusion.2
  861.1 4.2 add_convert_fusion
  865.3 4.1 all-to-all-start
  870.6 72.0 %all-to-all-done = bf16[4,128,2048]{2,1,0:T(8,128)(2,1)S(1)} async-done(((bf16[4,128,2048]{2,1,0:T(8,128)(2,1)}), bf16[4,128,2048]{2,1,0:T(8,128)(2,1)S(1)}, u32[]{:S(2)}, u32[]{:S(2)}) %all-to-all-start) | async-done | bytes 2097184 | tf_op jit(solution)/shard_map/all_to_all | solution.py:56
  943.1 1.0 add_convert_fusion.3
  944.1 2.0 multiply_subtract_fusion.3
  946.1 607.6 %all-reduce.3.cloned.1.call-done = f32[3,2048,512]{2,0,1:T(4,128)} async-done(((f32[3,2048,512]{2,0,1:T(4,128)}), f32[3,2048,512]{2,0,1:T(4,128)}) %all-reduce.3.cloned.1.call-update) | async-done | bytes 12582928
  1553.7 1.1 constant_dynamic-slice_fusion.1
  1554.9 2.4 multiply_subtract_fusion.2
  1557.3 361.8 %reduce-scatter.8.cloned.1.call-done = f32[64,2048]{1,0:T(8,128)} async-done(((f32[2048,2048]{1,0:T(8,128)}), f32[64,2048]{1,0:T(8,128)}) %reduce-scatter.8.cloned.1.call-update) | async-done | bytes 524304 | tf_op jit(solution)/shard_map/reduce_scatter | solution.py:326
  1919.1 2.4 multiply_subtract_fusion.1
  1921.6 382.3 %reduce-scatter.10.cloned.1.call-done = f32[64,2061]{1,0:T(8,128)} async-done(((f32[2048,2061]{1,0:T(8,128)}), f32[64,2061]{1,0:T(8,128)}) %reduce-scatter.10.cloned.1.call-update) | async-done | bytes 527632
  2303.9 0.8 slice.141
  2305.4 4.5 all-to-all-start.2
  2309.9 2.4 multiply_subtract_fusion
  2312.3 2.9 all-to-all-done.2
  (170 shorter events, 12.5 us)
Async XLA Ops:
  7.2 4.4 copy-start.29
  7.2 4.4 copy-start.6
  7.2 4.5 copy-start.8
  7.2 5.5 copy-start.46
  7.2 44.2 %all-gather.5.cloned.1.call-start = ((), (), s32[]{:S(2)}) async-start(), calls=%async_computation.7 | async-start | bytes 5242880 | tf_op jit(solution)/shard_map/all_gather | solution.py:27
  9.7 588.1 %all-gather.3.cloned.1.call-start = ((), (), s32[]{:S(2)}) async-start(), calls=%async_computation.6 | async-start | bytes 26492928 | tf_op jit(solution)/shard_map/all_gather | solution.py:38
  11.7 0.9 copy-start.18
  12.7 931.4 %reduce-scatter.6.cloned.1.call-start = ((), (), s32[]{:S(2)}) async-start(), calls=%async_computation.8 | async-start | bytes 4325376 | tf_op jit(solution)/shard_map/reduce_scatter | solution.py:325
  53.4 563.8 %copy-start.42 = (f32[512]{0:T(512)}, f32[512]{0:T(512)S(1)}, u32[]{:S(2)}) copy-start(f32[512]{0:T(512)S(1)} %broadcast_multiply_fusion) | copy-start | bytes 6148
  55.7 561.6 %copy-start.44 = (f32[512]{0:T(512)}, f32[512]{0:T(512)S(1)}, u32[]{:S(2)}) copy-start(f32[512]{0:T(512)S(1)} %add_rsqrt_fusion) | copy-start | bytes 6148
  602.0 15.3 copy-start.38
  629.6 3.7 copy-start.19
  629.7 3.7 copy-start.21
  629.7 3.7 copy-start.30
  629.7 3.7 copy-start.32
  629.7 3.1 copy-start.3
  629.7 4.5 copy-start
  633.4 0.8 copy-start.4
  637.5 916.2 %all-reduce.3.cloned.1.call-start = ((), (), s32[]{:S(2)}) async-start(), calls=%async_computation.11 | async-start | bytes 33554432
  641.5 0.8 copy-start.15
  645.7 2.5 copy-start.14
  645.7 2.5 copy-start.20
  645.7 2.5 copy-start.22
  647.6 1.8 copy-start.28
  647.6 1.8 copy-start.31
  647.6 1.8 copy-start.33
  648.2 2.1 copy-start.23
  650.7 3.7 copy-start.10
  650.7 3.7 copy-start.39
  650.8 3.7 copy-start.43
  650.8 3.7 copy-start.45
  654.5 8.7 copy-start.11
  681.1 0.9 copy-start.37
  681.1 1238.0 %reduce-scatter.8.cloned.1.call-start = ((), (), s32[]{:S(2)}) async-start(), calls=%async_computation.9 | async-start | bytes 17301504 | tf_op jit(solution)/shard_map/reduce_scatter | solution.py:326
  682.0 18.9 copy-start.1
  709.1 1.3 copy-start.49
  719.1 1.0 copy-start.12
  720.1 5.7 copy-start.2
  720.1 5.7 copy-start.50
  735.5 56.5 %all-to-all-start.1 = ((bf16[4,128,2048]{2,1,0:T(8,128)(2,1)}), bf16[4,128,2048]{2,1,0:T(8,128)(2,1)S(1)}, u32[]{:S(2)}, u32[]{:S(2)}) async-start(bf16[4,128,2048]{2,1,0:T(8,128)(2,1)} %bitcast.94), calls=%async_computation.1 | async-start | bytes 4194304 | tf_op jit(solution)/shard_map/all_to_all | solution.py:56
  739.7 1564.2 %reduce-scatter.10.cloned.1.call-start = ((), (), s32[]{:S(2)}) async-start(), calls=%async_computation.10 | async-start | bytes 18382848
  754.2 39.8 %copy-start.13 = (bf16[128,2048]{1,0:T(8,128)(2,1)S(1)}, bf16[128,2048]{1,0:T(8,128)(2,1)}, u32[]{:S(2)}) copy-start(bf16[128,2048]{1,0:T(8,128)(2,1)} %param.19) | copy-start | bytes 1572868
  852.4 1.6 copy-start.48
  854.0 7.0 copy-start.5
  865.3 4.1 copy-start.47
  865.3 77.8 %copy-start.16 = (bf16[128,2048]{1,0:T(8,128)(2,1)S(1)}, bf16[128,2048]{1,0:T(8,128)(2,1)}, u32[]{:S(2)}) copy-start(bf16[128,2048]{1,0:T(8,128)(2,1)} %param.18) | copy-start | bytes 1572868
  865.3 77.8 %copy-start.34 = (f32[2048]{0:T(1024)S(1)}, f32[2048]{0:T(1024)}, u32[]{:S(2)}) copy-start(f32[2048]{0:T(1024)} %get-tuple-element.165) | copy-start | bytes 24580
  865.3 77.8 %copy-start.35 = (f32[2048]{0:T(1024)S(1)}, f32[2048]{0:T(1024)}, u32[]{:S(2)}) copy-start(f32[2048]{0:T(1024)} %get-tuple-element.166) | copy-start | bytes 24580
  865.3 77.3 %all-to-all-start = ((bf16[4,128,2048]{2,1,0:T(8,128)(2,1)}), bf16[4,128,2048]{2,1,0:T(8,128)(2,1)S(1)}, u32[]{:S(2)}, u32[]{:S(2)}) async-start(bf16[4,128,2048]{2,1,0:T(8,128)(2,1)} %bitcast.18), calls=%async_computation | async-start | bytes 4194304 | tf_op jit(solution)/shard_map/all_to_all | solution.py:56
  869.4 685.5 %copy-start.17 = (f32[3,64,512]{2,1,0:T(8,128)S(1)}, f32[3,64,512]{2,1,0:T(8,128)}, u32[]{:S(2)}) copy-start(f32[3,64,512]{2,1,0:T(8,128)} %param.21) | copy-start | bytes 1179652
  943.1 976.1 %copy-start.7 = (f32[64,2048]{1,0:T(8,128)S(1)}, f32[64,2048]{1,0:T(8,128)}, u32[]{:S(2)}) copy-start(f32[64,2048]{1,0:T(8,128)} %param.23) | copy-start | bytes 1572868
  943.1 976.1 %copy-start.24 = (f32[64,2048]{1,0:T(8,128)S(1)}, f32[64,2048]{1,0:T(8,128)}, u32[]{:S(2)}) copy-start(f32[64,2048]{1,0:T(8,128)} %param.30) | copy-start | bytes 1572868
  943.1 976.1 %copy-start.25 = (f32[64,2048]{1,0:T(8,128)S(1)}, f32[64,2048]{1,0:T(8,128)}, u32[]{:S(2)}) copy-start(f32[64,2048]{1,0:T(8,128)} %param.31) | copy-start | bytes 1572868
  944.1 1365.8 %copy-start.9 = (f32[2048,64]{0,1:T(8,128)S(1)}, f32[2048,64]{0,1:T(8,128)}, u32[]{:S(2)}) copy-start(f32[2048,64]{0,1:T(8,128)} %param.24) | copy-start | bytes 1572868
  944.1 1365.8 %copy-start.26 = (f32[2048,64]{0,1:T(8,128)S(1)}, f32[2048,64]{0,1:T(8,128)}, u32[]{:S(2)}) copy-start(f32[2048,64]{0,1:T(8,128)} %param.32) | copy-start | bytes 1572868
  944.1 1365.8 %copy-start.27 = (f32[2048,64]{0,1:T(8,128)S(1)}, f32[2048,64]{0,1:T(8,128)}, u32[]{:S(2)}) copy-start(f32[2048,64]{0,1:T(8,128)} %param.33) | copy-start | bytes 1572868
  1557.3 759.3 %copy-start.36 = (f32[13,64]{1,0:T(8,128)S(1)}, f32[13,64]{1,0:T(8,128)}, u32[]{:S(2)}) copy-start(f32[13,64]{1,0:T(8,128)} %param.25) | copy-start | bytes 9988
  1557.3 759.3 %copy-start.40 = (f32[13,64]{1,0:T(8,128)S(1)}, f32[13,64]{1,0:T(8,128)}, u32[]{:S(2)}) copy-start(f32[13,64]{1,0:T(8,128)} %param.34) | copy-start | bytes 9988
  1557.3 759.3 %copy-start.41 = (f32[13,64]{1,0:T(8,128)S(1)}, f32[13,64]{1,0:T(8,128)}, u32[]{:S(2)}) copy-start(f32[13,64]{1,0:T(8,128)} %param.35) | copy-start | bytes 9988
  2305.4 9.8 all-to-all-start.2
Sparse Core Ops, SparseCore 0:
  10.3 41.1 all-gather.4
  53.1 544.6 all-gather.2
  637.7 171.6 reduce-scatter.5
  811.7 741.9 all-reduce.2
  1556.0 363.1 reduce-scatter.7
  1921.4 382.4 reduce-scatter.9
where the time goes:
time: 2330 us; the launch traced here: 2320 us
  waiting for transfers between devices  2040 us (88%)
  local copies, waits for them, and re-layouts  112 us (5%)
  matrix products  105 us (5%)
  other arithmetic  34.7 us (1%)
    unnamed x8, waiting for transfers between devices  990 us
    all_gather x1, waiting for transfers between devices, turned_gather(): filled = lax.all_gather(both, axis, axis=0, tiled=True)  542 us
    reduce_scatter x1, waiting for transfers between devices, local(): lax.psum_scatter(up_grad, 'dp', scatter_dimension=0, tiled=True)  362 us
    all_to_all x2, waiting for transfers between devices, summed_on_arrival(): lax.all_to_all(parts, axis, split_axis=0, concat_axis=0, tiled=True)  110 us
  transfers between devices with their start and end apart: 9, of which 8 were waited for; matrix products, arithmetic and copies ran while one was open for 9% of the time, Pallas kernels for 0%

commit v1 on v0

v1 whole, which is shorter than its diff:
```python
import functools
import math

import jax
import jax.numpy as jnp
from jax import lax
from jax.experimental import pallas as pl
from jax.experimental.pallas import tpu as pltpu
from jax.sharding import PartitionSpec as P

HD = 256
ROT = 64
UPDATE_STEP = 10
RING_SIZE = 4


norm_eps = 1e-05
beta_first = 0.9
beta_second = 0.95
adam_eps = 1e-08
matrix_rate = 0.02
vector_rate = 0.2
matrix_decay = 0.01
masked_score = -1e30
inv_root_two = 1.0 / math.sqrt(2.0)
inv_root_tau = 1.0 / math.sqrt(2.0 * math.pi)

MESH = pl.DeviceIdType.MESH
ANY = pl.BlockSpec(memory_space=pl.ANY)
VMEM = pl.BlockSpec(memory_space=pltpu.VMEM)


def place():
    dp, tensor = lax.axis_index("dp"), lax.axis_index("tensor")
    z = (tensor // 2) * 2 + dp % 2
    return dp // 8, (dp // 2) % RING_SIZE, z, tensor % 2


def device(y, x, z, core):
    return ((y * RING_SIZE + x) * 2 + z % 2, (z // 2) * 2 + core)


def around(i, step):
    return (i + step + RING_SIZE) % RING_SIZE


def greet(devices):
    barrier = pltpu.get_barrier_semaphore()
    for d in devices:
        pl.semaphore_signal(barrier, inc=1, device_id=d, device_id_type=MESH)


def meet(devices):
    pl.semaphore_wait(pltpu.get_barrier_semaphore(), len(devices))


def mailbox(note, send, recv, *lead):
    def post(k, src, dst, to):
        note[0] = (id(send), *lead, k)
        return pltpu.make_async_remote_copy(
            src_ref=src,
            dst_ref=dst,
            send_sem=send.at[(*lead, k)],
            recv_sem=recv.at[(*lead, k)],
            device_id=to,
            device_id_type=MESH,
        )

    return post


LOW = jnp.bfloat16
WIDE = jnp.float32
GROUP = 512
TILE = 256
WIDE_PART, REST = slice(0, 768), slice(768, 1280)
LANES = 128
PLANE_MESSAGES = 33
RING_MESSAGES = 8


VEC, UP, QKV, OD = range(4)
DY = 3
(
    SWAP,
    OWN,
    OTHER,
    ROUND_ONE_X,
    ROUND_ONE_Y,
    ROUND_TWO_A,
    ROUND_TWO_B,
    ROUND_TWO_C,
    ROUND_THREE,
    LAST_ROUND,
    RING,
    RING_ON,
    RING_FAR,
    TABLES,
    VECTORS_X,
    VECTORS_Y,
    VECTORS,
    NORM,
    FETCH,
    HIDDEN,
    PROJECT,
    ATTEND,
    OD_GRADS,
) = range(23)
(
    FIRST,
    NEAR,
    SECOND,
    FAR_SIDE,
    FINISH,
    Z_MATE,
    Z_FIRST,
    Z_SECOND,
    Z_FINISH,
    LOADS,
    VEC_ONE,
    VEC_TWO,
    VEC_THREE,
    SETTLE,
    CAT_GRADS,
    UP_GRADS,
    BRANCH,
    ATTEND_BACK,
    QKV_GRADS,
    NORM_GRADS,
) = range(20)
FORWARD_ORDER = (
    (OWN, UP), (SWAP, UP), (SWAP, QKV), (SWAP, VEC), (RING, 0), (OWN, QKV), (OTHER, UP),
    (VECTORS_X,), (OTHER, QKV), (VECTORS_Y,), (SWAP, OD), (ROUND_ONE_X, UP), (ROUND_ONE_Y, UP),
    (TABLES,), (ROUND_ONE_X, QKV), (ROUND_ONE_Y, QKV), (VECTORS,), (RING_ON, 0),
    (ROUND_TWO_A, UP), (RING, 1), (ROUND_TWO_B, UP), (NORM, 0), (ROUND_TWO_C, UP), (NORM, 4),
    (NORM, 2), (ROUND_THREE, UP), (RING_FAR, 0), (NORM, 1), (ROUND_TWO_B, QKV), (OTHER, OD),
    (NORM, 6), (LAST_ROUND, UP), (FETCH, UP), (OWN, OD), (HIDDEN, 0), (ROUND_TWO_A, QKV),
    (ROUND_TWO_C, QKV), (RING_ON, 1), (HIDDEN, 1), (ROUND_THREE, QKV), (ROUND_ONE_Y, OD),
    (HIDDEN, 2), (ROUND_ONE_X, OD), (HIDDEN, 3), (RING_FAR, 1), (LAST_ROUND, QKV),
    (ROUND_TWO_A, OD), (FETCH, QKV), (PROJECT, 0), (PROJECT, 1), (ATTEND, 0), (FETCH, DY),
    (ROUND_TWO_B, OD), (ATTEND, 1), (ROUND_TWO_C, OD), (OD_GRADS, 0), (ROUND_THREE, OD),
    (OD_GRADS, 1), (OD_GRADS, 2), (OD_GRADS, 3), (LAST_ROUND, OD),
)
BACKWARD_ORDER = (
    (FIRST, OD), (LOADS,), (CAT_GRADS, 0), (CAT_GRADS, 1), (CAT_GRADS, 2), (CAT_GRADS, 3),
    (UP_GRADS, 0), (UP_GRADS, 1), (UP_GRADS, 2), (UP_GRADS, 3), (FIRST, UP), (BRANCH, 0),
    (NEAR, OD, 0), (BRANCH, 1), (Z_MATE, 0), (NEAR, OD, 1), (BRANCH, 2), (BRANCH, 3),
    (ATTEND_BACK, 0), (Z_MATE, 1), (Z_FIRST, 0), (ATTEND_BACK, 1), (QKV_GRADS, 0), (QKV_GRADS, 1),
    (QKV_GRADS, 2), (Z_FIRST, 1), (Z_SECOND, 0), (QKV_GRADS, 3), (FIRST, QKV), (NEAR, UP, 0),
    (NORM_GRADS, 0), (NORM_GRADS, 1), (Z_MATE, 3), (Z_MATE, 2), (Z_SECOND, 1), (NORM_GRADS, 2),
    (Z_FINISH, 0), (Z_FIRST, 3), (NEAR, UP, 1), (NORM_GRADS, 3), (Z_FIRST, 2), (SECOND, OD, 1),
    (Z_SECOND, 3), (Z_MATE, 5), (SECOND, UP, 0), (VEC_ONE,), (NEAR, QKV, 1), (FAR_SIDE, OD, 1),
    (Z_SECOND, 2), (Z_MATE, 4), (Z_FIRST, 5), (SECOND, UP, 1), (FINISH, OD, 1), (NEAR, QKV, 0),
    (Z_FIRST, 4), (Z_FINISH, 1), (FAR_SIDE, UP, 0), (Z_SECOND, 5), (VEC_TWO,), (SECOND, OD, 0),
    (FAR_SIDE, UP, 1), (VEC_THREE,), (Z_FINISH, 3), (SECOND, QKV, 1), (Z_SECOND, 4),
    (SECOND, QKV, 0), (FAR_SIDE, OD, 0), (FINISH, UP, 1), (FAR_SIDE, QKV, 1), (FAR_SIDE, QKV, 0),
    (FINISH, QKV, 1), (Z_FINISH, 2), (FINISH, QKV, 0), (FINISH, OD, 0), (SETTLE,),
    (FINISH, UP, 0), (Z_FINISH, 5), (Z_FINISH, 4),
)


def wide(v):
    return v.astype(WIDE)


def nn(a, b):
    return jnp.dot(a, b, preferred_element_type=WIDE)


def nt(a, b):
    return lax.dot_general(a, b, (((1,), (1,)), ((), ())), preferred_element_type=WIDE)


def turn_over(eye, v):
    return nt(eye[...], v).astype(LOW)


def fill_eye(eye):
    row = lax.broadcasted_iota(jnp.int32, eye.shape, 0)
    eye[...] = wide(row == lax.broadcasted_iota(jnp.int32, eye.shape, 1)).astype(LOW)


def cols(k, size):
    return pl.ds(pl.multiple_of(k * size, size), size)


def turned(v, cos_table, sin_table):
    first = v[:, :LANES]
    lane = lax.broadcasted_iota(jnp.int32, first.shape, 1)
    swapped = jnp.where(
        lane < ROT // 2,
        pltpu.roll(first, LANES - ROT // 2, 1),
        pltpu.roll(first, ROT // 2, 1),
    )
    return jnp.concatenate([first * cos_table + swapped * sin_table, v[:, LANES:]], axis=1)


def soft_columns(query, key, start, first):
    scores = nt(key, query) * (HD**-0.5)
    key_at = lax.broadcasted_iota(jnp.int32, scores.shape, 0)
    query_at = lax.broadcasted_iota(jnp.int32, scores.shape, 1) + first
    allowed = (wide(key_at) >= start) & (key_at <= query_at)
    scores = jnp.where(allowed, scores, masked_score)
    powers = jnp.exp(scores - jnp.max(scores, axis=0, keepdims=True))
    return powers * (1.0 / jnp.sum(powers, axis=0, keepdims=True))


def streamed(count, copies, use):
    for c in copies(0, 0):
        c.start()

    @pl.loop(0, count)
    def _(k):
        slot = lax.rem(k, 2)

        @pl.when(k + 1 < count)
        def _():
            for c in copies(k + 1, 1 - slot):
                c.start()

        for c in copies(k, slot):
            c.wait()
        use(k, slot)


def play(order, loops, act):
    at = 0
    while at < len(order):
        kind = order[at][0]
        if kind not in loops:
            act(*order[at])
            at += 1
            continue
        hooks, due = {}, []
        end = max(k for k, entry in enumerate(order) if entry[0] == kind)
        for entry in order[at + 1 : end + 1]:
            if entry[0] == kind:
                if due:
                    hooks[entry[1]] = due
                due = []
            else:
                due.append(entry)
        loops[kind](hooks)
        at = end + 1


def forward_kernel(
    x_in, dy_in, lengths, vectors_in, up_in, qkv_in, out_in, down_in,
    dy_out, up_out, qkv_out, od_out, vecs_out, one_out, two_out, unit_out, heads_out, cat_out,
    slope_out, turn_out, soft_out, grad_out,
    xv, len_v, vec_w, one, two, unit, dy_v, up_w, qkv_w, cat, slope, heads, turn, flip_one, flip_two, stage,
    pre_one, pre_two, soft, begin, eye, len_in, vec_s, up_s, qkv_s, od_s, up_f, qkv_f, out_f, down_f,
    send, recv, ring_send, ring_recv, len_sems, local_sems, keep_sems, stage_sems, wide_sems,
):
    y, x, z, core = place()
    zl = z % 2
    tensor = (z // 2) * 2 + core
    head = tensor * 2 + zl
    other = 1 - zl
    partner = device(y, x, z + 1 - 2 * zl, core)
    xp, xm, yp, ym = around(x, 1), around(x, -1), around(y, 1), around(y, -1)
    zp, zm = around(z, 1), around(z, -1)
    xo, yo, zo = around(x, 2), around(y, 2), around(z, 2)
    to_xp, to_xm = device(y, xp, z, core), device(y, xm, z, core)
    to_yp, to_ym = device(yp, x, z, core), device(ym, x, z, core)
    to_zp, to_zm = device(y, x, zp, core), device(y, x, zm, core)
    mate = device(y, x, z, 1 - core)
    line_x = (to_xp, device(y, xo, z, core), to_xm)
    line_y = (to_yp, device(yo, x, z, core), to_ym)
    neighbours = [*line_x, *line_y, to_zp, to_zm, mate]
    greet(neighbours)

    wide_copies = [
        pltpu.make_async_copy(src, dst, wide_sems.at[k])
        for k, (src, dst) in enumerate(
            ((up_in, up_f), (qkv_in, qkv_f), (out_in, out_f), (down_in, down_f))
        )
    ]
    for c in wide_copies:
        c.start()
    for r in range(4):
        len_in[r : r + 1, :] = jnp.full((1, LANES), lengths[0, r].astype(WIDE))
    len_in[4:8, :] = jnp.zeros((4, LANES), WIDE)
    fill_eye(eye)
    vec_s[...] = jnp.zeros(vec_s.shape, WIDE)
    vec = wide(vectors_in[...].astype(LOW))
    for h in range(2):
        vec_s[h, 0 : vec.shape[0], 0 : vec.shape[1]] = vec

    def prepare(i):
        if i == UP:
            wide_copies[0].wait()
            n = up_s.shape[-1]
            for h in range(2):
                up_s[h] = up_f[:, h * n : (h + 1) * n].astype(LOW)
        elif i == QKV:
            wide_copies[1].wait()
            for h in range(2):
                for c in range(3):
                    at = slice(c * HD, (c + 1) * HD)
                    qkv_s[h, :, at] = qkv_f[c, :, h * HD : (h + 1) * HD].astype(LOW)
        else:
            wide_copies[2].wait()
            wide_copies[3].wait()
            n = od_s.shape[-1] - HD
            for h in range(2):
                od_s[h, :, 0:HD] = out_f[:, h * HD : (h + 1) * HD].astype(LOW)
                od_s[h, :, HD:] = down_f[:, h * n : (h + 1) * n].astype(LOW)

    w_in = (vec_s, up_s, qkv_s, od_s)
    w_out = (vec_w, up_out, qkv_out, od_out)
    started, note = {}, [None]

    def go(make):
        make().start()
        started[note[0]] = make

    def own_copy(k):
        if k < 4:
            src, dst = w_in[k].at[zl], w_out[k].at[y, x, zl]
        elif k < 6:
            src, dst = rings[k - 4][0], rings[k - 4][1].at[zl, tensor]
        else:
            src, dst = len_in, len_v.at[zl]
        return pltpu.make_async_copy(src, dst, local_sems.at[k])

    rings = ((x_in, xv), (dy_in, dy_out))
    for k in (VEC, 4, 5, 6):
        own_copy(k).start()
    for i in (UP, QKV, OD):
        prepare(i)
        own_copy(i).start()
    meet(neighbours)

    posts = [mailbox(note, send, recv, i) for i in range(4)]
    ring_posts = [mailbox(note, ring_send, ring_recv, j) for j in range(2)]
    four = (to_xp, to_xm, to_yp, to_ym)

    def slot_of(ref, zz, cc):
        return ref.at[zz % 2, (zz // 2) * 2 + cc]

    def arrived(i, k, ref):
        posts[i](k, ref, ref, mate).wait_recv()

    def ring_arrived(j, k, ref):
        ring_posts[j](k, ref, ref, mate).wait_recv()

    def halves_of(blk):
        n = blk.shape[0] // 2
        return blk.at[pl.ds(0, n)], blk.at[pl.ds(n, n)]

    def swap(i):
        go(lambda: posts[i](32, w_in[i].at[other], w_out[i].at[y, x, zl], partner))

    def own_half(i):
        for d in range(4):
            go(lambda d=d: posts[i](d, w_in[i].at[zl], w_out[i].at[y, x, zl], four[d]))

    def other_half(i):
        mine = lambda: w_out[i].at[y, x, other]
        arrived(i, 32, mine())
        for d in range(4):
            go(lambda d=d: posts[i](4 + d, mine(), mine(), four[d]))

    def round_one_x(i):
        w = w_out[i]
        blk = lambda: w.at[y, xm, zl]
        arrived(i, 0, blk())
        go(lambda blk=blk: posts[i](8, halves_of(blk())[0], halves_of(blk())[0], to_xp))
        go(lambda blk=blk: posts[i](12, blk(), blk(), to_yp))
        go(lambda blk=blk: posts[i](13, blk(), blk(), to_ym))
        blk = lambda: w.at[y, xp, zl]
        arrived(i, 1, blk())
        go(lambda blk=blk: posts[i](9, halves_of(blk())[1], halves_of(blk())[1], to_xm))
        go(lambda blk=blk: posts[i](14, blk(), blk(), to_yp))
        go(lambda blk=blk: posts[i](15, blk(), blk(), to_ym))

    def round_one_y(i):
        w = w_out[i]
        blk = lambda: w.at[ym, x, other]
        arrived(i, 6, blk())
        go(lambda blk=blk: posts[i](10, halves_of(blk())[0], halves_of(blk())[0], to_yp))
        go(lambda blk=blk: posts[i](18, blk(), blk(), to_xp))
        go(lambda blk=blk: posts[i](19, blk(), blk(), to_xm))
        blk = lambda: w.at[yp, x, other]
        arrived(i, 7, blk())
        go(lambda blk=blk: posts[i](11, halves_of(blk())[1], halves_of(blk())[1], to_ym))
        go(lambda blk=blk: posts[i](20, blk(), blk(), to_xp))
        go(lambda blk=blk: posts[i](21, blk(), blk(), to_xm))

    def round_two_a(i):
        w = w_out[i]
        blk = lambda: w.at[ym, x, zl]
        arrived(i, 2, blk())
        go(lambda blk=blk: posts[i](24, blk(), blk(), to_yp))
        blk = lambda: w.at[y, xm, other]
        arrived(i, 4, blk())
        go(lambda blk=blk: posts[i](28, blk(), blk(), to_xp))

    def round_two_b(i):
        w = w_out[i]
        blk = lambda: w.at[y, xo, zl]
        arrived(i, 8, halves_of(blk())[0])
        arrived(i, 9, halves_of(blk())[1])
        go(lambda blk=blk: posts[i](16, blk(), blk(), to_yp))
        go(lambda blk=blk: posts[i](17, blk(), blk(), to_ym))
        blk = lambda: w.at[yo, x, other]
        arrived(i, 10, halves_of(blk())[0])
        arrived(i, 11, halves_of(blk())[1])
        go(lambda blk=blk: posts[i](22, blk(), blk(), to_xp))
        go(lambda blk=blk: posts[i](23, blk(), blk(), to_xm))

    def round_two_c(i):
        w = w_out[i]
        blk = lambda: w.at[ym, xm, zl]
        arrived(i, 12, blk())
        go(lambda blk=blk: posts[i](25, blk(), blk(), to_yp))
        blk = lambda: w.at[yp, xp, zl]
        arrived(i, 15, blk())
        go(lambda blk=blk: posts[i](26, blk(), blk(), to_ym))
        blk = lambda: w.at[ym, xm, other]
        arrived(i, 18, blk())
        go(lambda blk=blk: posts[i](29, blk(), blk(), to_xp))
        blk = lambda: w.at[yp, xp, other]
        arrived(i, 21, blk())
        go(lambda blk=blk: posts[i](30, blk(), blk(), to_xm))

    def round_three(i):
        w = w_out[i]
        blk = lambda: w.at[yp, xo, zl]
        arrived(i, 17, blk())
        go(lambda blk=blk: posts[i](27, blk(), blk(), to_ym))
        blk = lambda: w.at[yo, xp, other]
        arrived(i, 23, blk())
        go(lambda blk=blk: posts[i](31, blk(), blk(), to_xm))

    def last_round(i):
        if i == OD:
            for key in list(started)[:-20]:
                started.pop(key)().wait_send()
        w = w_out[i]
        arrived(i, 3, w.at[yp, x, zl])
        arrived(i, 5, w.at[y, xp, other])
        arrived(i, 13, w.at[yp, xm, zl])
        arrived(i, 14, w.at[ym, xp, zl])
        arrived(i, 16, w.at[ym, xo, zl])
        arrived(i, 19, w.at[ym, xp, other])
        arrived(i, 20, w.at[yp, xm, other])
        arrived(i, 22, w.at[yo, xm, other])
        arrived(i, 24, w.at[yo, x, zl])
        arrived(i, 25, w.at[yo, xm, zl])
        arrived(i, 26, w.at[yo, xp, zl])
        arrived(i, 27, w.at[yo, xo, zl])
        arrived(i, 28, w.at[y, xo, other])
        arrived(i, 29, w.at[ym, xo, other])
        arrived(i, 30, w.at[yp, xo, other])
        arrived(i, 31, w.at[yo, xo, other])

    def ring_own(j):
        a, b = rings[j]
        for k, to in enumerate((to_zp, to_zm, mate)):
            go(lambda k=k, to=to: ring_posts[j](k, a, slot_of(b, z, core), to))

    def ring_on(j):
        b = rings[j][1]
        blk = lambda: slot_of(b, zm, core)
        ring_arrived(j, 0, blk())
        go(lambda blk=blk: ring_posts[j](3, halves_of(blk())[0], halves_of(blk())[0], to_zp))
        go(lambda blk=blk: ring_posts[j](5, blk(), blk(), mate))
        blk = lambda: slot_of(b, zp, core)
        ring_arrived(j, 1, blk())
        go(lambda blk=blk: ring_posts[j](4, halves_of(blk())[1], halves_of(blk())[1], to_zm))
        go(lambda blk=blk: ring_posts[j](6, blk(), blk(), mate))

    def ring_far(j):
        blk = lambda: slot_of(rings[j][1], zo, core)
        ring_arrived(j, 3, halves_of(blk())[0])
        ring_arrived(j, 4, halves_of(blk())[1])
        go(lambda blk=blk: ring_posts[j](7, blk(), blk(), mate))

    def ring_last(j):
        b = rings[j][1]
        ring_arrived(j, 2, slot_of(b, z, 1 - core))
        ring_arrived(j, 5, slot_of(b, zm, 1 - core))
        ring_arrived(j, 6, slot_of(b, zp, 1 - core))
        ring_arrived(j, 7, slot_of(b, zo, 1 - core))

    kept = {}

    def keep(k, src, dst):
        make = lambda: pltpu.make_async_copy(src, dst, keep_sems.at[k])
        make().start()
        kept[k] = make

    def fetch(k, src, dst):
        fetched[k] = lambda: pltpu.make_async_copy(src, dst, local_sems.at[7 + k])
        fetched[k]().start()

    def fetch_for(i):
        if i == UP:
            own_copy(UP).wait()
            fetch(0, up_out, up_w)
        elif i == QKV:
            own_copy(QKV).wait()
            fetch(1, qkv_out, qkv_w)
        else:
            own_copy(5).wait()
            ring_last(1)
            fetch(2, dy_out, dy_v)

    def tables():
        lengths_copy().wait_recv()
        own_copy(6).wait()

        @pl.loop(0, 8)
        def _(k):
            g, part = k // 4, k % 4
            shape = (LANES, LANES)
            row = wide(lax.broadcasted_iota(jnp.int32, shape, 0) + part * LANES)
            lane = lax.broadcasted_iota(jnp.int32, shape, 1)
            start = jnp.zeros(shape, WIDE)
            end = jnp.zeros((1, LANES), WIDE)
            for s in range(4):
                end = end + len_v[g, s : s + 1, :]
                start = jnp.where(row >= end, jnp.broadcast_to(end, shape), start)
            half_rot = ROT // 2
            step = wide(lane % half_rot) * (-2.0 * math.log(10000.0) / ROT)
            angle = (row - start) * jnp.exp(step)
            sine = jnp.sin(angle)
            rows = cols(k, LANES)
            turn[0, rows] = jnp.where(lane < ROT, jnp.cos(angle), 1.0)
            turn[1, rows] = jnp.where(lane < half_rot, -sine, jnp.where(lane < ROT, sine, 0.0))

        for g in range(2):
            column = wide(lax.broadcasted_iota(jnp.int32, (1, GROUP), 1))
            start = jnp.zeros((1, GROUP), WIDE)
            end = jnp.zeros((1, LANES), WIDE)
            for r in range(4):
                end = end + len_v[g, r : r + 1, :]
                ends = jnp.concatenate([end] * (GROUP // LANES), axis=1)
                start = jnp.where(column >= ends, ends, start)
            begin[g : g + 1, :] = start

        keep(0, turn, turn_out)

    def vectors_x():
        own_copy(VEC).wait()
        arrived(VEC, 32, vec_w.at[y, x, other])
        for k in range(3):
            go(lambda k=k: posts[VEC](k, vec_w.at[y, x], vec_w.at[y, x], line_x[k]))

    def vectors_y():
        for k in range(3):
            arrived(VEC, k, vec_w.at[y, x])
        for k in range(3):
            go(lambda k=k: posts[VEC](3 + k, vec_w.at[y], vec_w.at[y], line_y[k]))

    def vectors():
        for k in range(3):
            arrived(VEC, 3 + k, vec_w.at[y])
        for p in range(RING_SIZE * RING_SIZE):
            lead, tail = vec_w[p // RING_SIZE, p % RING_SIZE, 0], vec_w[p // RING_SIZE, p % RING_SIZE, 1]
            vecs_out[:, p * LANES : (p + 1) * LANES] = lead + pltpu.roll(tail, LANES // 2, 1)

    def norm(zz, cc):
        b = (zz % 2) * RING_SIZE + (zz // 2) * 2 + cc

        @pl.loop(0, 4)
        def _(k):
            v = wide(xv[zz % 2, (zz // 2) * 2 + cc, cols(k, 32)])
            centred = v - jnp.mean(v, axis=-1, keepdims=True)
            var = jnp.mean(centred * centred, axis=-1, keepdims=True)
            u = centred * lax.rsqrt(var + norm_eps)
            to = cols(b * 4 + k, 32)
            unit[to] = u.astype(LOW)
            one[to] = (u * vecs_out[0:1, :] + vecs_out[1:2, :]).astype(LOW)
            two[to] = (u * vecs_out[2:3, :] + vecs_out[3:4, :]).astype(LOW)

    def norms(k):
        if k == 0:
            own_copy(4).wait()
            norm(z, core)
        elif k == 1:
            ring_arrived(0, 2, slot_of(xv, z, 1 - core))
            norm(z, 1 - core)
        elif k == 2:
            norm(zm, core)
            norm(zp, core)
        elif k == 4:
            ring_arrived(0, 5, slot_of(xv, zm, 1 - core))
            norm(zm, 1 - core)
            ring_arrived(0, 6, slot_of(xv, zp, 1 - core))
            norm(zp, 1 - core)
        else:
            norm(zo, core)
            ring_arrived(0, 7, slot_of(xv, zo, 1 - core))
            norm(zo, 1 - core)

    def at_step(hooks, k):
        for due, entries in hooks.items():

            @pl.when(k == due)
            def _():
                for entry in entries:
                    act(*entry)

    def keep_rows():
        if 1 not in kept:
            keep(1, one, one_out)
            keep(2, two, two_out)
            keep(3, unit, unit_out)

    def gelu(pre, m, n):
        size = pre.shape[1]
        rows = pl.ds(m * GROUP, GROUP)
        at = pl.ds(pl.multiple_of(n * size + TILE, TILE), size)
        hidden = pre[...]
        cdf = 0.5 * (1.0 + lax.erf(hidden * inv_root_two))
        cat[rows, at] = (hidden * cdf).astype(LOW)
        bell = hidden * jnp.exp(-0.5 * hidden * hidden) * inv_root_tau
        slope[rows, at] = (cdf + bell).astype(LOW)

    def hidden_tiles(hooks):
        keep_rows()
        fetched[0]().wait()
        size = pre_one.shape[1]
        last = up_w.shape[-1] // size

        @pl.loop(0, last)
        def _(n):
            w = up_w[:, :, :, :, cols(n, size)].reshape(-1, size)
            bias = vecs_out[pl.ds(9 + head // 2, 1), cols((head % 2) * last + n, size)]
            at_step(hooks, 2 * n)
            gelu(pre_two, 1, (n + last - 1) % last)
            pre_one[...] = nn(two[0:GROUP], w) + bias
            at_step(hooks, 2 * n + 1)
            gelu(pre_one, 0, n)
            pre_two[...] = nn(two[GROUP:], w) + bias

        gelu(pre_two, 1, last - 1)
        slope[:, 0:TILE] = jnp.ones((2 * GROUP, TILE), LOW)
        keep(4, slope, slope_out)

    def project(hooks):
        keep_rows()
        fetched[1]().wait()

        @pl.loop(0, 2)
        def _(m):
            at_step(hooks, m)
            rows = cols(m, GROUP)
            all_three = nn(one[rows], qkv_w[...].reshape(-1, 3 * HD))
            for c in range(3):
                pre = all_three[:, c * HD : (c + 1) * HD] + vecs_out[4 + c : 5 + c, cols(head, HD)]
                if c < 2:
                    pre = turned(pre, turn[0, rows], turn[1, rows])
                heads[c, rows] = pre.astype(LOW)

        keep(5, heads, heads_out)

    def attend(hooks):
        @pl.loop(0, 2)
        def _(g):
            at_step(hooks, g)
            for part in range(2):
                rows, keys = cols(2 * g + part, TILE), pl.ds(cols(g, GROUP).start, (part + 1) * TILE)
                start = begin[pl.ds(g, 1), part * TILE : (part + 1) * TILE]
                columns = soft_columns(heads[0, rows], heads[1, keys], start, part * TILE)
                columns = columns.astype(LOW)
                soft[g, part, 0 : (part + 1) * TILE] = columns
                cat[rows, 0:HD] = nn(turn_over(eye, columns), heads[2, keys]).astype(LOW)

        keep(7, soft, soft_out)

    def od_grads(hooks):
        keep(6, cat, cat_out)
        fetched[2]().wait()
        flips = (flip_one, flip_two)

        def flip(to, k, e):
            tile = dy_v[:, :, :, cols(2 * k + e, TILE)].reshape(-1, TILE)
            to[e * TILE : (e + 1) * TILE, :] = turn_over(eye, tile)

        def staged(k, half):
            return pltpu.make_async_copy(stage.at[half], grad_out.at[k], stage_sems.at[half])

        for e in range(2):
            flip(flip_one, 0, e)

        @pl.loop(0, 2)
        def _(kk):
            for half in range(2):
                k = 2 * kk + half
                at_step(hooks, k)

                @pl.when(kk > 0)
                def _():
                    staged(k - 2, half).wait()

                for part, at in enumerate((WIDE_PART, REST)):
                    res = nn(flips[half][...], cat[:, at]).astype(LOW)
                    flip(flips[1 - half], (k + 1) % RING_SIZE, part)
                    stage[half, :, :, :, at] = res.reshape(RING_SIZE, 2, -1, at.stop - at.start)

                staged(k, half).start()

        for half in range(2):
            staged(2 + half, half).wait()

    fetched = {}
    def lengths_copy():
        return pltpu.make_async_remote_copy(
            src_ref=len_in,
            dst_ref=len_v.at[zl],
            send_sem=len_sems.at[0],
            recv_sem=len_sems.at[1],
            device_id=partner,
            device_id_type=MESH,
        )

    moves = {
        SWAP: swap,
        OWN: own_half,
        OTHER: other_half,
        ROUND_ONE_X: round_one_x,
        ROUND_ONE_Y: round_one_y,
        ROUND_TWO_A: round_two_a,
        ROUND_TWO_B: round_two_b,
        ROUND_TWO_C: round_two_c,
        ROUND_THREE: round_three,
        LAST_ROUND: last_round,
        RING: ring_own,
        RING_ON: ring_on,
        RING_FAR: ring_far,
        TABLES: tables,
        VECTORS_X: vectors_x,
        VECTORS_Y: vectors_y,
        VECTORS: vectors,
        NORM: norms,
        FETCH: fetch_for,
    }

    def act(kind, *args):
        moves[kind](*args)

    loops = {HIDDEN: hidden_tiles, PROJECT: project, ATTEND: attend, OD_GRADS: od_grads}
    lengths_copy().start()
    play(FORWARD_ORDER, loops, act)
    own_copy(3).wait()
    lengths_copy().wait_send()
    for make in started.values():
        make().wait_send()
    for make in kept.values():
        make().wait()


def forward(rows, cot, lengths, vectors, weights):
    tokens, model = rows.shape
    total = 2 * RING_SIZE * tokens
    up, qkv, out_w, down = weights
    owned = up.shape[0]
    widths = (LANES, up.shape[1] // 2, 3 * HD, (out_w.shape[1] + down.shape[1]) // 2)
    halves = [(2, 16, LANES), *((2, owned, w) for w in widths[1:])]
    plane = [(RING_SIZE, RING_SIZE, *h) for h in halves]
    cat_cols = widths[3]
    shape = jax.ShapeDtypeStruct
    out = [
        shape((2, RING_SIZE, tokens, model), LOW),
        shape(plane[1], LOW),
        shape(plane[2], LOW),
        shape(plane[3], LOW),
        shape((16, model), WIDE),
        shape((total, model), LOW),
        shape((total, model), LOW),
        shape((total, model), LOW),
        shape((3, total, HD), LOW),
        shape((total, cat_cols), LOW),
        shape((total, cat_cols), LOW),
        shape((2, total, LANES), WIDE),
        shape((2, 2, GROUP, TILE), LOW),
        shape(plane[3], LOW),
    ]
    specs = [VMEM if k == 4 else ANY for k in range(len(out))]
    return pl.pallas_call(
        forward_kernel,
        out_shape=out,
        in_specs=[ANY, ANY, pl.BlockSpec(memory_space=pltpu.SMEM), VMEM, ANY, ANY, ANY, ANY],
        out_specs=specs,
        scratch_shapes=[
            pltpu.VMEM((2, RING_SIZE, tokens, model), LOW),
            pltpu.VMEM((2, 8, LANES), WIDE),
            pltpu.VMEM(plane[0], WIDE),
            pltpu.VMEM((total, model), LOW),
            pltpu.VMEM((total, model), LOW),
            pltpu.VMEM((total, model), LOW),
            pltpu.VMEM((2, RING_SIZE, tokens, model), LOW),
            pltpu.VMEM(plane[1], LOW),
            pltpu.VMEM(plane[2], LOW),
            pltpu.VMEM((total, cat_cols), LOW),
            pltpu.VMEM((total, cat_cols), LOW),
            pltpu.VMEM((3, total, HD), LOW),
            pltpu.VMEM((2, total, LANES), WIDE),
            pltpu.VMEM((GROUP, total), LOW),
            pltpu.VMEM((GROUP, total), LOW),
            pltpu.VMEM((2, RING_SIZE, 2, owned, cat_cols), LOW),
            pltpu.VMEM((GROUP, GROUP), WIDE),
            pltpu.VMEM((GROUP, GROUP), WIDE),
            pltpu.VMEM((2, 2, GROUP, TILE), LOW),
            pltpu.VMEM((8, GROUP), WIDE),
            pltpu.VMEM((TILE, TILE), LOW),
            pltpu.VMEM((8, LANES), WIDE),
            pltpu.VMEM(halves[0], WIDE),
            *(pltpu.VMEM(h, LOW) for h in halves[1:]),
            *(pltpu.VMEM(w.shape, WIDE) for w in weights),
            pltpu.SemaphoreType.DMA((4, PLANE_MESSAGES)),
            pltpu.SemaphoreType.DMA((4, PLANE_MESSAGES)),
            pltpu.SemaphoreType.DMA((2, RING_MESSAGES)),
            pltpu.SemaphoreType.DMA((2, RING_MESSAGES)),
            pltpu.SemaphoreType.DMA((2,)),
            pltpu.SemaphoreType.DMA((10,)),
            pltpu.SemaphoreType.DMA((8,)),
            pltpu.SemaphoreType.DMA((2,)),
            pltpu.SemaphoreType.DMA((4,)),
        ],
        compiler_params=pltpu.CompilerParams(
            collective_id=0, has_side_effects=True, vmem_limit_bytes=62 * 2**20
        ),
        name="forward_and_gather",
    )(rows, cot, lengths, vectors, *weights)


def backward_kernel(
    dy_in, up_in, qkv_in, od_in, vecs, one_in, two_in, unit_in, heads_in, cat_in, slope_in,
    turn_in, soft_in, od_grad,
    own_od_out, own_up_out, own_qkv_out, swap_od, swap_up, swap_qkv, vec_out, u_zero_out, u_one_out,
    own_od, own_up, own_qkv, u_zero, u_one,
    up_grad, qkv_grad, dcat, cat, heads, turn, soft, flip_one, flip_two, vecg, vec_block,
    od_near, od_me, od_full, tiles, eye,
    part_zero, both_zero, zfar_zero, znear_zero, part_one, both_one, zfar_one, znear_one,
    far_od, near_od, far2_od, near2_od, out_od,
    far_up, near_up, far2_up, near2_up, out_up,
    far_qkv, near_qkv, far2_qkv, near2_qkv, out_qkv,
    vec_x, vec_y, vec_z, vec_row, vec_own,
    send, recv, z_send, z_recv, v_send, v_recv, load_sems, stream_sems, out_sems,
):
    y, x, z, core = place()
    zl = z % 2
    head = ((z // 2) * 2 + core) * 2 + zl
    other = 1 - zl
    partner = device(y, x, z + 1 - 2 * zl, core)
    xp, xm, yp, ym = around(x, 1), around(x, -1), around(y, 1), around(y, -1)
    zp, zm = around(z, 1), around(z, -1)
    xo, yo, zo = around(x, 2), around(y, 2), around(z, 2)
    to_x = (device(y, xp, z, core), device(y, xm, z, core))
    to_y = (device(yp, x, z, core), device(ym, x, z, core))
    to_z = (partner, device(y, x, around(z, 2 * zl - 1), core))
    mate = device(y, x, z, 1 - core)
    line_x = (to_x[0], device(y, xo, z, core), to_x[1])
    line_y = (to_y[0], device(yo, x, z, core), to_y[1])
    line_z = [mate]
    for k in (1, 2, 3):
        for c in (0, 1):
            line_z.append(device(y, x, around(z, k), (core + c) % 2))
    neighbours = [*line_x, *line_y, *line_z]
    greet(neighbours)

    def load(k, src, dst):
        copy = pltpu.make_async_copy(src, dst, load_sems.at[k])
        copy.start()
        return copy

    half_model = part_zero.shape[-1]
    loads = [load(0, slope_in, dcat)]
    for c in range(2):
        at = slice(c * half_model, (c + 1) * half_model)
        loads.append(load(1 + c, dy_in.at[:, :, :, :, at], part_zero.at[c]))
    od_loads = [load(13 + k, od_in.at[k], od_full.at[k]) for k in range(RING_SIZE)]
    near_loads = []
    for way, half in enumerate((zl, other)):
        for d in range(2):
            two = pl.ds(2 * d, 2)
            src = (two, (xp, xm)[d], half) if way == 0 else ((yp, ym)[d], two, half)
            near_loads.append(load(3 + 2 * way + d, od_grad.at[src], od_near.at[way, d]))
        every = pl.ds(0, RING_SIZE)
        src = (every, x, half) if way == 0 else (y, every, half)
        near_loads.append(load(7 + way, od_grad.at[src], od_me.at[way]))
    late = [
        load(9, heads_in, heads),
        load(10, turn_in, turn),
        load(11, cat_in, cat),
        load(12, soft_in, soft),
    ]
    meet(neighbours)

    started, note = {}, [None]

    def go(make):
        make().start()
        started[note[0]] = make

    g_ref = {OD: od_grad, UP: up_grad, QKV: qkv_grad}
    bufs = {
        OD: (far_od, near_od, far2_od, near2_od, out_od, own_od, swap_od),
        UP: (far_up, near_up, far2_up, near2_up, out_up, own_up, swap_up),
        QKV: (far_qkv, near_qkv, far2_qkv, near2_qkv, out_qkv, own_qkv, swap_qkv),
    }
    posts = {i: mailbox(note, send, recv, i - 1) for i in (UP, QKV, OD)}
    z_posts = [mailbox(note, z_send, z_recv, j) for j in range(6)]
    v_post = mailbox(note, v_send, v_recv)

    def arrived(i, k, ref):
        posts[i](k, ref, ref, mate).wait_recv()

    def z_arrived(j, k, ref):
        z_posts[j](k, ref, ref, mate).wait_recv()

    halves = (zl, other)
    first_to, second_to = (to_x, to_y), (to_y, to_x)
    first = ((xp, xm, xo, x), (yp, ym, yo, y))
    second = ((yp, ym, yo, y), (xp, xm, xo, x))
    pair = (pl.ds(0, 2), pl.ds(2, 2))
    part_rows = (pl.ds(0, 32), pl.ds(32, 32))

    def block(i, way, along, across):
        if way == 0:
            return g_ref[i].at[across, along, halves[0]]
        return g_ref[i].at[along, across, halves[1]]

    def near_value(i, way, d, k):
        if i == OD:
            return od_near[way, d, k]
        return block(i, way, first[way][d], k + 2 * d)[...]

    def me_value(i, way, k, rows):
        if i == OD:
            return od_me[way, k, rows]
        return block(i, way, first[way][3], k).at[rows][...]

    def send_first(i):
        far, near = bufs[i][:2]
        for way in range(2):
            for d in range(2):
                go(
                    lambda way=way, d=d: posts[i](
                        way * 12 + d,
                        block(i, way, first[way][2], pair[d]),
                        far.at[way, d],
                        first_to[way][d],
                    )
                )
        for way in range(2):
            for d in range(2):
                go(
                    lambda way=way, d=d: posts[i](
                        way * 12 + 2 + d,
                        block(i, way, first[way][d], pair[1 - d]),
                        near.at[way, d, pair[1 - d]],
                        first_to[way][d],
                    )
                )

    def send_near(i, way):
        far, near = bufs[i][:2]
        for d in range(2):
            arrived(i, way * 12 + d, far.at[way, d])
            for k in range(2):
                far[way, d, k] = far[way, d, k] + near_value(i, way, d, k)
            go(
                lambda d=d: posts[i](
                    way * 12 + 4 + d, far.at[way, d], near.at[way, d, pair[d]], first_to[way][d]
                )
            )

    def send_second(i, way):
        far, near, far_two, near_two = bufs[i][:4]
        for d in range(2):
            arrived(i, way * 12 + 2 + d, near.at[way, d, pair[1 - d]])
            arrived(i, way * 12 + 4 + d, near.at[way, d, pair[d]])

        @pl.loop(0, 2 * RING_SIZE)
        def _(t):
            k, rows = t // 2, cols(t % 2, 32)
            total = near[way, 0, k, rows] + near[way, 1, k, rows]
            near[way, 0, k, rows] = total + me_value(i, way, k, rows)

        for d in range(2):
            go(
                lambda d=d: posts[i](
                    way * 12 + 6 + d,
                    near.at[way, 0, second[way][2], part_rows[d]],
                    far_two.at[way, d],
                    second_to[way][d],
                )
            )
        for d in range(2):
            go(
                lambda d=d: posts[i](
                    way * 12 + 8 + d,
                    near.at[way, 0, second[way][d], part_rows[1 - d]],
                    near_two.at[way, d, part_rows[1 - d]],
                    second_to[way][d],
                )
            )

    def send_last(i, way):
        far, near, far_two, near_two = bufs[i][:4]
        for d in range(2):
            arrived(i, way * 12 + 6 + d, far_two.at[way, d])
            rows = part_rows[d]
            far_two[way, d] = far_two[way, d] + near[way, 0, second[way][d], rows]
            go(
                lambda d=d: posts[i](
                    way * 12 + 10 + d,
                    far_two.at[way, d],
                    near_two.at[way, d, part_rows[d]],
                    second_to[way][d],
                )
            )

    def finish(i, way):
        near, near_two, out, mine, swapped = (bufs[i][k] for k in (1, 3, 4, 5, 6))
        for d in range(2):
            arrived(i, way * 12 + 8 + d, near_two.at[way, d, part_rows[1 - d]])
            arrived(i, way * 12 + 10 + d, near_two.at[way, d, part_rows[d]])
        total = wide(near[way, 0, second[way][3]]) + wide(near_two[way, 0]) + wide(near_two[way, 1])
        if way == 1:
            out[...] = total.astype(LOW)
            go(lambda: posts[i](24, out, swapped, partner))
        else:
            mine[...] = total.astype(LOW)
            out_copy(i - 1).start()

    def z_bufs(j):
        if j < 2:
            return [r.at[j] for r in (part_zero, both_zero, zfar_zero, znear_zero)]
        return [r.at[j - 2] for r in (part_one, both_one, zfar_one, znear_one)]

    def z_rows(j):
        lead = 64 if j < 2 else 16
        return pl.ds(0, lead), pl.ds(lead, near_rows - lead)

    near_rows = znear_zero.shape[2]
    z_ends = (z + 1 - 2 * zl, around(z, 2 * zl - 1))

    def z_to_mate(j):
        go(lambda: z_posts[j](0, z_bufs(j)[0].at[:, :, 1 - core], z_bufs(j)[1], mate))

    def z_block(j, zz):
        return z_bufs(j)[1].at[zz % 2, zz // 2]

    def z_first(j):
        part, both, far, near = z_bufs(j)
        z_arrived(j, 0, both)

        @pl.loop(0, 8)
        def _(k):
            b, c, rows = k // 4, (k // 2) % 2, cols(k % 2, 64)
            both[b, c, rows] = both[b, c, rows] + part[b, c, core, rows]

        rows = z_rows(j)
        for d in range(2):
            go(
                lambda d=d: z_posts[j](
                    1 + d, z_block(j, zo).at[rows[d]], z_bufs(j)[2].at[rows[d]], to_z[d]
                )
            )
        for d in range(2):
            go(
                lambda d=d: z_posts[j](
                    3 + d,
                    z_block(j, z_ends[d]).at[rows[d]],
                    z_bufs(j)[3].at[d, rows[d]],
                    to_z[d],
                )
            )

    def z_second(j):
        part, both, far, near = z_bufs(j)
        rows = z_rows(j)
        for d in range(2):
            z_arrived(j, 1 + d, far.at[rows[d]])
            zz = z_ends[1 - d]
            far[rows[d]] = far[rows[d]] + both[zz % 2, zz // 2, rows[d]]
            go(
                lambda d=d: z_posts[j](
                    6 - d, z_bufs(j)[2].at[rows[d]], z_bufs(j)[3].at[1 - d, rows[d]], to_z[1 - d]
                )
            )

    def z_finish(j):
        part, both, far, near = z_bufs(j)
        rows = z_rows(j)
        for d in range(2):
            z_arrived(j, 3 + d, near.at[d, rows[d]])
            z_arrived(j, 5 + d, near.at[d, rows[1 - d]])
        out, at = (u_zero, j) if j < 2 else (u_one, j - 2)
        width = near.shape[-1]
        for k in range(2):
            rows = pl.ds(64 * k, 64)
            total = wide(both[zl, z // 2, rows]) + wide(near[0, rows]) + wide(near[1, rows])
            out[rows, at * width : (at + 1) * width] = total.astype(LOW)
        out_copy(3 + j).start()

    def at_step(hooks, k):
        for due, entries in hooks.items():

            @pl.when(k == due)
            def _():
                for entry in entries:
                    act(*entry)

    def out_copy(k):
        if k < 3:
            src, dst = ((own_up, own_up_out), (own_qkv, own_qkv_out), (own_od, own_od_out))[k]
        else:
            j = k - 3
            src, dst = (u_zero, u_zero_out) if j < 2 else (u_one, u_one_out)
            width = src.shape[1] // (2 if j < 2 else 4)
            at = pl.ds((j if j < 2 else j - 2) * width, width)
            src, dst = src.at[:, at], dst.at[:, at]
        return pltpu.make_async_copy(src, dst, out_sems.at[k])

    def cat_grads(hooks):
        for c in od_loads:
            c.wait()
        thirds = (slice(0, 512), slice(512, 1024), slice(1024, 1280))
        for step, (m, at) in enumerate(((m, at) for at in thirds for m in range(2))):
            for entry in hooks.get(step, ()):
                act(*entry)
            w = od_full[:, :, :, :, at].reshape(-1, at.stop - at.start)
            rows = pl.ds(m * GROUP, GROUP)
            grad = nn(part_zero[0, m].reshape(GROUP, -1), w[:half_model])
            grad = grad + nn(part_zero[1, m].reshape(GROUP, -1), w[half_model:])
            dcat[rows, at] = (grad * wide(dcat[rows, at])).astype(LOW)

    def weight_grads(hooks, sem, source, rights, to, bias):
        flips = (flip_one, flip_two)
        size = to.shape[-1] // len(rights)

        def copy(k, half):
            at = stream_sems.at[sem, half]
            return pltpu.make_async_copy(source.at[:, cols(k, GROUP)], tiles.at[half], at)

        def flip(half, e):
            at = slice(e * TILE, (e + 1) * TILE)
            flips[half][at, :] = turn_over(eye, tiles[half, :, at])

        for half in range(2):
            copy(half, half).start()
        copy(0, 0).wait()

        for e in range(2):
            flip(0, e)

        @pl.loop(0, 2)
        def _(kk):
            for half in range(2):
                k = 2 * kk + half
                at_step(hooks, k)
                if half == 0:
                    copy(k + 1, 1).wait()
                else:

                    @pl.when(kk == 0)
                    def _():
                        copy(k + 1, 0).wait()

                @pl.when(kk == 0)
                def _():
                    copy(k + 2, half).start()

                for n, right in enumerate(rights):
                    res = nn(flips[half][...], right[...])
                    row, at = bias(n)
                    vecg[row, at] = res[GROUP : GROUP + 1]
                    part = res[0:GROUP].astype(LOW)
                    to[k, :, :, :, n * size : (n + 1) * size] = part.reshape(RING_SIZE, 2, -1, size)
                for e in range(2):
                    flip(1 - half, e)

    def attend_back(hooks):
        @pl.loop(0, 2)
        def _(g):
            at_step(hooks, g)
            dkey, dvalue = [], []
            for part in range(2):
                rows, count = cols(2 * g + part, TILE), (part + 1) * TILE
                keys = pl.ds(cols(g, GROUP).start, count)
                columns = soft[g, part, 0:count]
                query, key, grad = heads[0, rows], heads[1, keys], dcat[rows, 0:HD]
                dsoft = nt(heads[2, keys], grad)
                inner = jnp.sum(wide(columns) * dsoft, axis=0, keepdims=True)
                dscore = (wide(columns) * (dsoft - inner)).astype(LOW)
                dquery = nn(turn_over(eye, dscore), key) * (HD**-0.5)
                heads[0, rows] = turned(dquery, turn[0, rows], -turn[1, rows]).astype(LOW)
                dkey.append(nn(dscore, query))
                dvalue.append(nn(columns, grad))
            for part in range(2):
                rows, at = cols(2 * g + part, TILE), slice(part * TILE, (part + 1) * TILE)
                whole_key, whole_value = dkey[1][at], dvalue[1][at]
                if part == 0:
                    whole_key, whole_value = whole_key + dkey[0], whole_value + dvalue[0]
                whole_key = turned(whole_key * (HD**-0.5), turn[0, rows], -turn[1, rows])
                heads[1, rows] = whole_key.astype(LOW)
                heads[2, rows] = whole_value.astype(LOW)

    def branch(hooks):
        @pl.loop(0, RING_SIZE)
        def _(k):
            at_step(hooks, k)
            w = od_full[k].reshape(GROUP, -1)
            for m in range(2):
                res = nt(cat[m * GROUP : (m + 1) * GROUP], w).astype(LOW)
                part_zero[k // 2, m, :, :, :, cols(k % 2, GROUP)] = res.reshape(2, 2, -1, GROUP)

    def norm_grads(hooks):
        up_at, qkv_at = slice(0, up_in.shape[-1]), slice(0, qkv_in.shape[-1])

        def copies(k, slot):
            return [
                pltpu.make_async_copy(
                    qkv_in.at[k], od_full.at[2 + slot, :, :, :, qkv_at], stream_sems.at[2, slot]
                ),
                pltpu.make_async_copy(
                    up_in.at[k], od_full.at[slot, :, :, :, up_at], stream_sems.at[3, slot]
                ),
                pltpu.make_async_copy(
                    unit_in.at[:, cols(k, GROUP)], tiles.at[slot], stream_sems.at[4, slot]
                ),
            ]

        def use(k, slot):
            at_step(hooks, k)
            w_one = od_full[2 + slot, :, :, :, qkv_at].reshape(GROUP, -1)
            w_two = od_full[slot, :, :, :, up_at].reshape(GROUP, -1)
            at = cols(k, GROUP)
            sums = [jnp.zeros((1, GROUP), WIDE)] * 4
            for part in range(4):
                m, inner = part // 2, part % 2
                rows = pl.ds(part * TILE, TILE)
                a = nt(heads[0, rows], w_one[:, 0:HD])
                for c in (1, 2):
                    a = a + nt(heads[c, rows], w_one[:, c * HD : (c + 1) * HD])
                b = nt(dcat[rows, TILE:], w_two)
                u = wide(tiles[slot, rows])
                res = (a * vecs[0:1, at] + b * vecs[2:3, at]).astype(LOW)
                part_one[k, m, inner] = res.reshape(2, -1, GROUP)
                new = (a * u, a, b * u, b)
                sums = [s + jnp.sum(v, axis=0, keepdims=True) for s, v in zip(sums, new)]
            for r in range(4):
                vecg[r : r + 1, at] = sums[r]

        streamed(RING_SIZE, copies, use)

    def vec_first():
        lane = lax.broadcasted_iota(jnp.int32, (16, LANES), 1)
        for p in range(RING_SIZE * RING_SIZE):
            v = vecg[:, p * LANES : (p + 1) * LANES]
            lead = jnp.where(lane < LANES // 2, v, 0.0)
            tail = jnp.where(lane < LANES // 2, pltpu.roll(v, LANES // 2, 1), 0.0)
            vec_block[p // RING_SIZE, p % RING_SIZE, 0] = lead
            vec_block[p // RING_SIZE, p % RING_SIZE, 1] = tail
        for k in range(3):
            go(lambda k=k: v_post(k, vec_block.at[:, around(x, k + 1)], vec_x.at[k], line_x[k]))

    def vec_second():
        for k in range(3):
            v_post(k, vec_x.at[k], vec_x.at[k], mate).wait_recv()
        for r in range(RING_SIZE):
            vec_row[r] = vec_block[r, x] + vec_x[0, r] + vec_x[1, r] + vec_x[2, r]
        for k in range(3):
            go(lambda k=k: v_post(3 + k, vec_row.at[around(y, k + 1)], vec_y.at[k], line_y[k]))

    def vec_third():
        for k in range(3):
            v_post(3 + k, vec_y.at[k], vec_y.at[k], mate).wait_recv()
        vec_own[...] = vec_row[y] + vec_y[0] + vec_y[1] + vec_y[2]
        for k in range(7):
            there = lambda k=k: zl if k == 0 else (z + (k + 1) // 2) % 2
            go(
                lambda k=k, there=there: v_post(
                    6 + k, vec_own.at[there()], vec_z.at[k], line_z[k]
                )
            )

    def vec_finish():
        total = vec_own[zl]
        for k in range(7):
            v_post(6 + k, vec_z.at[k], vec_z.at[k], mate).wait_recv()
            total = total + vec_z[k]
        vec_out[...] = total

    def wait_loads():
        vecg[...] = jnp.zeros(vecg.shape, WIDE)
        fill_eye(eye)
        for ref in (flip_one, flip_two):
            ref[GROUP:, :] = jnp.ones((16, ref.shape[1]), LOW)
        for c in loads:
            c.wait()
        for c in range(2):
            total = jnp.sum(wide(part_zero[c, zl, z // 2, core]), axis=0, keepdims=True)
            for r in (7, 8):
                vecg[r : r + 1, c * half_model : (c + 1) * half_model] = total

    def up_weight_grads(hooks):
        for c in near_loads:
            c.wait()
        def bias(n):
            return pl.ds(9 + head // 2, 1), cols((head % 2) * 2 + n, GROUP)

        rights = [dcat.at[:, TILE + n * GROUP : TILE + (n + 1) * GROUP] for n in range(2)]
        weight_grads(hooks, 5, two_in, rights, up_grad, bias)
        for c in late:
            c.wait()

    def qkv_weight_grads(hooks):
        def bias(n):
            return pl.ds(4 + n, 1), cols(head, HD)

        weight_grads(hooks, 6, one_in, [heads.at[c] for c in range(3)], qkv_grad, bias)

    def settle():
        for key in list(started)[:-20]:
            started.pop(key)().wait_send()

    moves = {
        SETTLE: settle,
        FIRST: send_first,
        NEAR: send_near,
        SECOND: send_second,
        FAR_SIDE: send_last,
        FINISH: finish,
        Z_MATE: z_to_mate,
        Z_FIRST: z_first,
        Z_SECOND: z_second,
        Z_FINISH: z_finish,
        LOADS: wait_loads,
        VEC_ONE: vec_first,
        VEC_TWO: vec_second,
        VEC_THREE: vec_third,
    }

    def act(kind, *args):
        moves[kind](*args)

    loops = {
        CAT_GRADS: cat_grads,
        UP_GRADS: up_weight_grads,
        BRANCH: branch,
        ATTEND_BACK: attend_back,
        QKV_GRADS: qkv_weight_grads,
        NORM_GRADS: norm_grads,
    }
    play(BACKWARD_ORDER, loops, act)
    vec_finish()
    for i in (UP, QKV, OD):
        arrived(i, 24, bufs[i][6])
    for k in range(9):
        out_copy(k).wait()
    for make in started.values():
        make().wait_send()


def backward(held):
    dy, up_full, qkv_full, od_full, vecs, one, two, unit, heads, cat, slope, turn, soft, _ = held
    total, model = one.shape
    tokens = dy.shape[2]
    owned = od_full.shape[3]
    widths = [w.shape[-1] for w in (od_full, up_full, qkv_full)]
    shape = jax.ShapeDtypeStruct
    out = [shape((owned, w), LOW) for w in widths]
    out += [shape((owned, w), LOW) for w in widths]
    out += [shape((16, LANES), WIDE)]
    out += [shape((tokens, model), LOW)] * 2
    plane = (RING_SIZE, RING_SIZE, 2, owned)
    scratch = [pltpu.VMEM((owned, w), LOW) for w in widths]
    scratch += [pltpu.VMEM((tokens, model), LOW)] * 2
    scratch += [
        pltpu.VMEM((*plane, widths[1]), LOW),
        pltpu.VMEM((*plane, widths[2]), LOW),
        pltpu.VMEM(slope.shape, LOW),
        pltpu.VMEM(cat.shape, LOW),
        pltpu.VMEM(heads.shape, LOW),
        pltpu.VMEM(turn.shape, WIDE),
        pltpu.VMEM(soft.shape, LOW),
        pltpu.VMEM((GROUP + 16, total), LOW),
        pltpu.VMEM((GROUP + 16, total), LOW),
        pltpu.VMEM((16, model), WIDE),
        pltpu.VMEM((RING_SIZE, RING_SIZE, 2, 16, LANES), WIDE),
        pltpu.VMEM((2, 2, 2, owned, widths[0]), LOW),
        pltpu.VMEM((2, RING_SIZE, owned, widths[0]), LOW),
        pltpu.VMEM((*plane, widths[0]), LOW),
        pltpu.VMEM((2, total, GROUP), LOW),
        pltpu.VMEM((TILE, TILE), LOW),
    ]
    for n in (2, 4):
        w = model // n
        scratch += [
            pltpu.VMEM((n, 2, 2, 2, tokens, w), LOW),
            pltpu.VMEM((n, 2, 2, tokens, w), LOW),
            pltpu.VMEM((n, tokens, w), LOW),
            pltpu.VMEM((n, 2, tokens, w), LOW),
        ]
    for w in widths:
        scratch += [
            pltpu.VMEM((2, 2, 2, owned, w), LOW),
            pltpu.VMEM((2, 2, RING_SIZE, owned, w), LOW),
            pltpu.VMEM((2, 2, owned // 2, w), LOW),
            pltpu.VMEM((2, 2, owned, w), LOW),
            pltpu.VMEM((owned, w), LOW),
        ]
    scratch += [
        pltpu.VMEM((3, RING_SIZE, 2, 16, LANES), WIDE),
        pltpu.VMEM((3, 2, 16, LANES), WIDE),
        pltpu.VMEM((7, 16, LANES), WIDE),
        pltpu.VMEM((RING_SIZE, 2, 16, LANES), WIDE),
        pltpu.VMEM((2, 16, LANES), WIDE),
        pltpu.SemaphoreType.DMA((3, 25)),
        pltpu.SemaphoreType.DMA((3, 25)),
        pltpu.SemaphoreType.DMA((6, 7)),
        pltpu.SemaphoreType.DMA((6, 7)),
        pltpu.SemaphoreType.DMA((13,)),
        pltpu.SemaphoreType.DMA((13,)),
        pltpu.SemaphoreType.DMA((17,)),
        pltpu.SemaphoreType.DMA((7, 2)),
        pltpu.SemaphoreType.DMA((9,)),
    ]
    specs = [VMEM if k == 4 else ANY for k in range(14)]
    return pl.pallas_call(
        backward_kernel,
        out_shape=out,
        in_specs=specs,
        out_specs=[VMEM if k == 6 else ANY for k in range(len(out))],
        scratch_shapes=scratch,
        compiler_params=pltpu.CompilerParams(
            collective_id=1, has_side_effects=True, vmem_limit_bytes=63 * 2**20
        ),
        name="backward_and_reduce",
    )(dy.reshape(2, 2, 2, tokens, model), *held[1:])


def adamw(weight, gradient, moment, square, step_rate, decay_rate):
    moment_new = beta_first * moment + (1.0 - beta_first) * gradient
    square_new = beta_second * square + (1.0 - beta_second) * gradient * gradient
    first_fix = 1.0 / (1.0 - beta_first**UPDATE_STEP)
    second_fix = 1.0 / (1.0 - beta_second**UPDATE_STEP)
    fixed = square_new * second_fix
    below = fixed * lax.rsqrt(fixed) + adam_eps
    inverse = pl.reciprocal(below, approx=True)
    inverse = inverse * (2.0 - below * inverse)
    direction = moment_new * first_fix * inverse
    weight_new = weight - step_rate * (direction + decay_rate * weight)
    return (weight_new, moment_new, square_new)


def update_kernel(*refs):
    (own_od, own_up, own_qkv, swap_od, swap_up, swap_qkv, vec_sum, u_zero, u_one, x_in, dy_in) = refs[:11]
    vecs, state, outs = refs[11], refs[12:27], refs[27:44]
    grads, rows_in, held = refs[44:50], refs[50:54], refs[54:69]
    block_v, grad_v, in_sems, out_sems = refs[69:]
    zl = lax.axis_index("dp") % 2
    started = []

    def load(src, dst):
        copy = pltpu.make_async_copy(src, dst, in_sems.at[len(started)])
        copy.start()
        started.append(copy)
        return copy

    stored = []

    def store(src, dst):
        copy = pltpu.make_async_copy(src, dst, out_sems.at[len(stored)])
        copy.start()
        stored.append(copy)

    sources = (own_od, own_up, own_qkv, swap_od, swap_up, swap_qkv)
    waits = {}
    for i, parts in ((2, (1, 4)), (0, (2, 5)), (1, (0, 3)), (3, ())):
        waits[i] = [load(sources[k], grads[k]) for k in parts]
        waits[i] += [load(state[3 * i + k], held[3 * i + k]) for k in range(3)]
    row_waits = [load(a, b) for a, b in zip((x_in, u_zero, u_one, dy_in), rows_in)]
    vec_waits = [load(state[12 + k], held[12 + k]) for k in range(3)]

    def new(i, at, gradient, rate, decay):
        three = held[3 * i : 3 * i + 3]
        weight, moment, square = (r[at] for r in three)
        for r, v in zip(three, adamw(weight, gradient, moment, square, rate, decay)):
            r[at] = v

    def done(i):
        for k in range(3):
            store(held[3 * i + k], outs[2 + 3 * i + k])

    def part(k, h, at):
        return wide(jnp.where(zl == h, grads[k][at], grads[k + 3][at]))

    def rows_of(k, size):
        return pl.ds(pl.multiple_of(k * size, size), size)

    for c in waits[2]:
        c.wait()

    @pl.loop(0, 4)
    def _(k):
        rows = rows_of(k, 16)
        for h in range(2):
            n = grads[1].shape[1]
            new(2, (rows, slice(h * n, (h + 1) * n)), part(1, h, (rows, slice(0, n))), matrix_rate, matrix_decay)

    done(2)
    for c in waits[0]:
        c.wait()
    for c in range(3):

        @pl.loop(0, 2)
        def _(k):
            rows = rows_of(k, 32)
            for h in range(2):
                g = part(2, h, (rows, slice(c * HD, (c + 1) * HD)))
                new(0, (c, rows, slice(h * HD, (h + 1) * HD)), g, matrix_rate, matrix_decay)

    done(0)
    for c in (*waits[1], *waits[3]):
        c.wait()

    @pl.loop(0, 4)
    def _(k):
        rows = rows_of(k, 16)
        n = grads[0].shape[1] - HD
        for h in range(2):
            g = part(0, h, (rows, slice(0, HD)))
            new(1, (rows, slice(h * HD, (h + 1) * HD)), g, matrix_rate, matrix_decay)
            g = part(0, h, (rows, slice(HD, HD + n)))
            new(3, (rows, slice(h * n, (h + 1) * n)), g, matrix_rate, matrix_decay)

    done(1)
    done(3)
    for c in (*row_waits, *vec_waits):
        c.wait()
    x_v, zero_v, one_v, dy_v = rows_in

    @pl.loop(0, 4)
    def _(k):
        rows = rows_of(k, 32)
        v = wide(x_v[rows])
        block_v[rows] = (v + wide(zero_v[rows]) + vecs[7:8, :] + vecs[8:9, :]).astype(LOW)
        centred = v - jnp.mean(v, axis=-1, keepdims=True)
        scale = lax.rsqrt(jnp.mean(centred * centred, axis=-1, keepdims=True) + norm_eps)
        unit = centred * scale
        g = wide(one_v[rows])
        g = g - jnp.mean(g, axis=-1, keepdims=True) - unit * jnp.mean(g * unit, axis=-1, keepdims=True)
        grad_v[rows] = wide(dy_v[rows]) + scale * g

    store(block_v, outs[0])
    store(grad_v, outs[1])
    at = (slice(None), slice(None))
    shape = held[12].shape
    new(4, at, vec_sum[0 : shape[0], 0 : shape[1]], vector_rate, 0.0)
    done(4)
    for c in stored:
        c.wait()


def update(reduced, rows, cot, vecs, state):
    own, vec_sum, sums = reduced[:6], reduced[6], reduced[7:]
    shape = jax.ShapeDtypeStruct
    out = [shape(rows.shape, LOW), shape(rows.shape, WIDE)]
    out += [shape(a.shape, WIDE) for a in state]
    scratch = [pltpu.VMEM(a.shape, a.dtype) for a in (*own, rows, *sums, cot, *state)]
    scratch += [
        pltpu.VMEM(rows.shape, LOW),
        pltpu.VMEM(rows.shape, WIDE),
        pltpu.SemaphoreType.DMA((25,)),
        pltpu.SemaphoreType.DMA((17,)),
    ]
    specs = [ANY] * 6 + [VMEM] + [ANY] * 4 + [VMEM] + [ANY] * 15
    return pl.pallas_call(
        update_kernel,
        out_shape=out,
        in_specs=specs,
        out_specs=[ANY] * len(out),
        scratch_shapes=scratch,
        compiler_params=pltpu.CompilerParams(vmem_limit_bytes=63 * 2**20),
        name="update",
    )(*own, vec_sum, *sums, rows, cot, vecs, *state)


def local(
    inputs,
    cotangent,
    lengths,
    qkv_weight,
    out_weight,
    up_weight,
    down_weight,
    norm_vectors,
    qkv_mean,
    qkv_square,
    out_mean,
    out_square,
    up_mean,
    up_square,
    down_mean,
    down_square,
    vector_mean,
    vector_square,
):
    weights = (up_weight, qkv_weight, out_weight.T, down_weight.T)
    held = forward(inputs, cotangent, lengths, norm_vectors, weights)
    state = (
        *(qkv_weight, qkv_mean, qkv_square),
        *(out_weight.T, out_mean.T, out_square.T),
        *(up_weight, up_mean, up_square),
        *(down_weight.T, down_mean.T, down_square.T),
        *(norm_vectors, vector_mean, vector_square),
    )
    out = list(update(backward(held), inputs, cotangent, held[4], state))
    for k in (5, 6, 7, 11, 12, 13):
        out[k] = out[k].T
    return tuple(out)


def solution(mesh):
    placed = (
        P(("dp", "tensor"), None),
        P(("dp", "tensor"), None),
        P("dp", None),
        P(None, "dp", "tensor"),
        P("tensor", "dp"),
        P("dp", "tensor"),
        P("tensor", "dp"),
        P(None, "dp"),
        P(None, "dp", "tensor"),
        P(None, "dp", "tensor"),
        P("tensor", "dp"),
        P("tensor", "dp"),
        P("dp", "tensor"),
        P("dp", "tensor"),
        P("tensor", "dp"),
        P("tensor", "dp"),
        P(None, "dp"),
        P(None, "dp"),
    )
    return jax.shard_map(
        local,
        mesh=mesh,
        in_specs=placed,
        out_specs=(
            P(("dp", "tensor"), None),
            P(("dp", "tensor"), None),
            P(None, "dp", "tensor"),
            P(None, "dp", "tensor"),
            P(None, "dp", "tensor"),
            P("tensor", "dp"),
            P("tensor", "dp"),
            P("tensor", "dp"),
            P("dp", "tensor"),
            P("dp", "tensor"),
            P("dp", "tensor"),
            P("tensor", "dp"),
            P("tensor", "dp"),
            P("tensor", "dp"),
            P(None, "dp"),
            P(None, "dp"),
            P(None, "dp"),
        ),
        check_vma=False,
    )
```

time: 2330 us -> 175 us (0.08)
  waiting for transfers between devices: 2040 us -> 0 us
  Pallas kernels: 0 us -> 174 us
  local copies, waits for them, and re-layouts: 112 us -> 0 us
  matrix products: 105 us -> 0 us
  other arithmetic: 34.7 us -> 0 us
    unnamed x8 -> x0, waiting for transfers between devices: 990 us -> none
    all_gather x2 -> x0, waiting for transfers between devices: 578 us -> none  [the longest x1 542 us: turned_gather(): filled = lax.all_gather(both, axis, axis=0, tiled=True)]
    reduce_scatter x2 -> x0, waiting for transfers between devices: 362 us -> none  [the longest x1 362 us: local(): lax.psum_scatter(up_grad, 'dp', scatter_dimension=0, tiled=True)]
    pallas_call x0 -> x3, Pallas kernels: none -> 174 us  [the longest x1 83.9 us: forward(): pl.pallas_call(forward_kernel, out_shape=out, in_specs=[ANY, ANY, pl.Bloc...]
    all_to_all x3 -> x0, waiting for transfers between devices: 113 us -> none  [the longest x2 110 us: summed_on_arrival(): lax.all_to_all(parts, axis, split_axis=0, concat_axis=0, tiled=True)]
    dot_general x18 -> x0, matrix products: 105 us -> none  [the longest x1 18.9 us: local(): jnp.dot(norm_two, up_full, preferred_element_type=jnp.float32) + up_bias]
    concatenate x4 -> x0, local copies, waits for them, and re-layouts: 40.1 us -> none  [the longest x1 38.7 us: sent_together(): both = jnp.concatenate(arrays, axis=along)]
    unnamed x116 -> x0, local copies, waits for them, and re-layouts: 29.1 us -> none
  transfers between devices with their start and end apart: 9 -> 0, of which waited for: 8 -> 0; matrix products, arithmetic and copies ran while one was open for 9% -> 0% of each run, Pallas kernels for 0% -> 0%
where the time goes in v1:
time: 175 us
  Pallas kernels  174 us (99%)
    pallas_call x1, Pallas kernels, forward(): pl.pallas_call(forward_kernel, out_shape=out, in_specs=[ANY, ANY, pl.Bloc...  83.9 us
    pallas_call x1, Pallas kernels, backward(): pl.pallas_call(backward_kernel, out_shape=out, in_specs=specs, out_specs=...  82.4 us
    pallas_call x1, Pallas kernels, update(): pl.pallas_call(update_kernel, out_shape=out, in_specs=specs, out_specs=[A...  7.9 us

profile of v1, /device:TPU:0, one launch (start us, length us, event | category | flops | bytes accessed | tf_op | source)
XLA Modules:
  0.0 175.0 jit_solution(18024803982184092338)
XLA Ops:
  0.7 83.9 %forward_and_gather.1 = (bf16[2,4,128,2048]{3,2,1,0:T(8,128)(2,1)}, bf16[4,4,2,64,1024]{4,3,2,1,0:T(8,128)(2,1)}, bf16[4,4,2,64,768]{4,3,2,1,0:T(8,128)(2,1)}, b...) custom-call(bf16[128,2048]{1,0:T(8,128)(2,1)} %refs_9_.1, ...), custom_call_target="tpu_custom_call" | custom-call | tf_op jit(solution)/shard_map/forward_and_gather/pallas_call | solution.py:784
  84.5 82.4 %backward_and_reduce.1 = (bf16[64,1280]{1,0:T(8,128)(2,1)}, bf16[64,1024]{1,0:T(8,128)(2,1)}, bf16[64,768]{1,0:T(8,128)(2,1)}, bf16[64,1280]{1,0:T(8,128)(2,1)},...) custom-call(bf16[2,2,2,128,2048]{4,3,2,1,0:T(8,128)(2,1)} %bitcast.1, ...), custom_call_target="tpu_custom_call" | custom-call | tf_op jit(solution)/shard_map/backward_and_reduce/pallas_call | solution.py:1429
  166.9 7.9 %update.1 = (bf16[128,2048]{1,0:T(8,128)(2,1)}, f32[128,2048]{1,0:T(8,128)}, f32[3,64,512]{2,1,0:T(8,128)}, f32[3,64,512]{2,1,0:T(8,128)}, f32[3,64,512]{2,1,0:T...) custom-call(bf16[64,1280]{1,0:T(8,128)(2,1)} %get-tuple-element.71.r, ...), custom_call_target="tpu_custom_call" | custom-call | tf_op jit(solution)/shard_map/update/pallas_call | solution.py:1578

commit v2 on v1

--- a/solution.py
+++ b/solution.py
@@ -143,19 +143,19 @@
 )
 BACKWARD_ORDER = (
     (FIRST, OD), (LOADS,), (CAT_GRADS, 0), (CAT_GRADS, 1), (CAT_GRADS, 2), (CAT_GRADS, 3),
-    (UP_GRADS, 0), (UP_GRADS, 1), (UP_GRADS, 2), (UP_GRADS, 3), (FIRST, UP), (BRANCH, 0),
-    (NEAR, OD, 0), (BRANCH, 1), (Z_MATE, 0), (NEAR, OD, 1), (BRANCH, 2), (BRANCH, 3),
-    (ATTEND_BACK, 0), (Z_MATE, 1), (Z_FIRST, 0), (ATTEND_BACK, 1), (QKV_GRADS, 0), (QKV_GRADS, 1),
-    (QKV_GRADS, 2), (Z_FIRST, 1), (Z_SECOND, 0), (QKV_GRADS, 3), (FIRST, QKV), (NEAR, UP, 0),
-    (NORM_GRADS, 0), (NORM_GRADS, 1), (Z_MATE, 3), (Z_MATE, 2), (Z_SECOND, 1), (NORM_GRADS, 2),
-    (Z_FINISH, 0), (Z_FIRST, 3), (NEAR, UP, 1), (NORM_GRADS, 3), (Z_FIRST, 2), (SECOND, OD, 1),
-    (Z_SECOND, 3), (Z_MATE, 5), (SECOND, UP, 0), (VEC_ONE,), (NEAR, QKV, 1), (FAR_SIDE, OD, 1),
-    (Z_SECOND, 2), (Z_MATE, 4), (Z_FIRST, 5), (SECOND, UP, 1), (FINISH, OD, 1), (NEAR, QKV, 0),
-    (Z_FIRST, 4), (Z_FINISH, 1), (FAR_SIDE, UP, 0), (Z_SECOND, 5), (VEC_TWO,), (SECOND, OD, 0),
-    (FAR_SIDE, UP, 1), (VEC_THREE,), (Z_FINISH, 3), (SECOND, QKV, 1), (Z_SECOND, 4),
-    (SECOND, QKV, 0), (FAR_SIDE, OD, 0), (FINISH, UP, 1), (FAR_SIDE, QKV, 1), (FAR_SIDE, QKV, 0),
-    (FINISH, QKV, 1), (Z_FINISH, 2), (FINISH, QKV, 0), (FINISH, OD, 0), (SETTLE,),
-    (FINISH, UP, 0), (Z_FINISH, 5), (Z_FINISH, 4),
+    (UP_GRADS, 0), (NEAR, OD, 1), (UP_GRADS, 1), (UP_GRADS, 2), (UP_GRADS, 3), (FIRST, UP),
+    (BRANCH, 0), (BRANCH, 1), (Z_MATE, 0), (BRANCH, 2), (BRANCH, 3), (Z_MATE, 1),
+    (ATTEND_BACK, 0), (Z_FIRST, 0), (NEAR, OD, 0), (ATTEND_BACK, 1), (QKV_GRADS, 0),
+    (Z_SECOND, 0), (QKV_GRADS, 1), (Z_FIRST, 1), (SECOND, OD, 1), (QKV_GRADS, 2), (QKV_GRADS, 3),
+    (FIRST, QKV), (NORM_GRADS, 0), (Z_MATE, 2), (Z_SECOND, 1), (FAR_SIDE, OD, 1), (NORM_GRADS, 1),
+    (Z_MATE, 3), (Z_FIRST, 2), (NEAR, UP, 0), (NEAR, UP, 1), (NORM_GRADS, 2), (Z_FIRST, 3),
+    (NEAR, QKV, 1), (Z_MATE, 4), (Z_SECOND, 2), (NORM_GRADS, 3), (Z_FINISH, 0), (FINISH, OD, 1),
+    (Z_FIRST, 4), (Z_MATE, 5), (SECOND, UP, 1), (VEC_ONE,), (SECOND, OD, 0), (Z_SECOND, 3),
+    (NEAR, QKV, 0), (SECOND, UP, 0), (Z_FIRST, 5), (Z_SECOND, 4), (FAR_SIDE, OD, 0),
+    (FAR_SIDE, UP, 1), (VEC_TWO,), (SECOND, QKV, 1), (Z_FINISH, 2), (Z_FINISH, 1), (VEC_THREE,),
+    (Z_SECOND, 5), (FAR_SIDE, UP, 0), (FINISH, UP, 1), (FAR_SIDE, QKV, 1), (SECOND, QKV, 0),
+    (FINISH, QKV, 1), (Z_FINISH, 3), (FINISH, UP, 0), (Z_FINISH, 4), (FINISH, OD, 0), (SETTLE,),
+    (FAR_SIDE, QKV, 0), (Z_FINISH, 5), (FINISH, QKV, 0),
 )
 
 
@@ -207,7 +207,7 @@
 
 def streamed(count, copies, use):
     for c in copies(0, 0):
-        c.start()
+        c.start(priority=1)
 
     @pl.loop(0, count)
     def _(k):
@@ -216,7 +216,7 @@
         @pl.when(k + 1 < count)
         def _():
             for c in copies(k + 1, 1 - slot):
-                c.start()
+                c.start(priority=1)
 
         for c in copies(k, slot):
             c.wait()
@@ -277,7 +277,7 @@
         )
     ]
     for c in wide_copies:
-        c.start()
+        c.start(priority=1)
     for r in range(4):
         len_in[r : r + 1, :] = jnp.full((1, LANES), lengths[0, r].astype(WIDE))
     len_in[4:8, :] = jnp.zeros((4, LANES), WIDE)
@@ -326,10 +326,10 @@
 
     rings = ((x_in, xv), (dy_in, dy_out))
     for k in (VEC, 4, 5, 6):
-        own_copy(k).start()
+        own_copy(k).start(priority=1)
     for i in (UP, QKV, OD):
         prepare(i)
-        own_copy(i).start()
+        own_copy(i).start(priority=1)
     meet(neighbours)
 
     posts = [mailbox(note, send, recv, i) for i in range(4)]
@@ -489,12 +489,12 @@
 
     def keep(k, src, dst):
         make = lambda: pltpu.make_async_copy(src, dst, keep_sems.at[k])
-        make().start()
+        make().start(priority=1)
         kept[k] = make
 
     def fetch(k, src, dst):
         fetched[k] = lambda: pltpu.make_async_copy(src, dst, local_sems.at[7 + k])
-        fetched[k]().start()
+        fetched[k]().start(priority=1)
 
     def fetch_for(i):
         if i == UP:
@@ -702,7 +702,7 @@
                     flip(flips[1 - half], (k + 1) % RING_SIZE, part)
                     stage[half, :, :, :, at] = res.reshape(RING_SIZE, 2, -1, at.stop - at.start)
 
-                staged(k, half).start()
+                staged(k, half).start(priority=1)
 
         for half in range(2):
             staged(2 + half, half).wait()
@@ -866,7 +866,7 @@
 
     def load(k, src, dst):
         copy = pltpu.make_async_copy(src, dst, load_sems.at[k])
-        copy.start()
+        copy.start(priority=1)
         return copy
 
     half_model = part_zero.shape[-1]
@@ -1028,7 +1028,7 @@
             go(lambda: posts[i](24, out, swapped, partner))
         else:
             mine[...] = total.astype(LOW)
-            out_copy(i - 1).start()
+            out_copy(i - 1).start(priority=1)
 
     def z_bufs(j):
         if j < 2:
@@ -1099,7 +1099,7 @@
             rows = pl.ds(64 * k, 64)
             total = wide(both[zl, z // 2, rows]) + wide(near[0, rows]) + wide(near[1, rows])
             out[rows, at * width : (at + 1) * width] = total.astype(LOW)
-        out_copy(3 + j).start()
+        out_copy(3 + j).start(priority=1)
 
     def at_step(hooks, k):
         for due, entries in hooks.items():
@@ -1146,7 +1146,7 @@
             flips[half][at, :] = turn_over(eye, tiles[half, :, at])
 
         for half in range(2):
-            copy(half, half).start()
+            copy(half, half).start(priority=1)
         copy(0, 0).wait()
 
         for e in range(2):
@@ -1167,7 +1167,7 @@
 
                 @pl.when(kk == 0)
                 def _():
-                    copy(k + 2, half).start()
+                    copy(k + 2, half).start(priority=1)
 
                 for n, right in enumerate(rights):
                     res = nn(flips[half][...], right[...])
@@ -1463,7 +1463,7 @@
 
     def load(src, dst):
         copy = pltpu.make_async_copy(src, dst, in_sems.at[len(started)])
-        copy.start()
+        copy.start(priority=len(started) % 2)
         started.append(copy)
         return copy
 
@@ -1471,15 +1471,15 @@
 
     def store(src, dst):
         copy = pltpu.make_async_copy(src, dst, out_sems.at[len(stored)])
-        copy.start()
+        copy.start(priority=len(stored) % 2)
         stored.append(copy)
 
     sources = (own_od, own_up, own_qkv, swap_od, swap_up, swap_qkv)
+    row_waits = [load(a, b) for a, b in zip((x_in, u_zero, u_one, dy_in), rows_in)]
     waits = {}
-    for i, parts in ((2, (1, 4)), (0, (2, 5)), (1, (0, 3)), (3, ())):
+    for i, parts in ((2, (1, 4)), (3, (0, 3)), (0, (2, 5)), (1, ())):
         waits[i] = [load(sources[k], grads[k]) for k in parts]
         waits[i] += [load(state[3 * i + k], held[3 * i + k]) for k in range(3)]
-    row_waits = [load(a, b) for a, b in zip((x_in, u_zero, u_one, dy_in), rows_in)]
     vec_waits = [load(state[12 + k], held[12 + k]) for k in range(3)]
 
     def new(i, at, gradient, rate, decay):
@@ -1498,45 +1498,7 @@
     def rows_of(k, size):
         return pl.ds(pl.multiple_of(k * size, size), size)
 
-    for c in waits[2]:
-        c.wait()
-
-    @pl.loop(0, 4)
-    def _(k):
-        rows = rows_of(k, 16)
-        for h in range(2):
-            n = grads[1].shape[1]
-            new(2, (rows, slice(h * n, (h + 1) * n)), part(1, h, (rows, slice(0, n))), matrix_rate, matrix_decay)
-
-    done(2)
-    for c in waits[0]:
-        c.wait()
-    for c in range(3):
-
-        @pl.loop(0, 2)
-        def _(k):
-            rows = rows_of(k, 32)
-            for h in range(2):
-                g = part(2, h, (rows, slice(c * HD, (c + 1) * HD)))
-                new(0, (c, rows, slice(h * HD, (h + 1) * HD)), g, matrix_rate, matrix_decay)
-
-    done(0)
-    for c in (*waits[1], *waits[3]):
-        c.wait()
-
-    @pl.loop(0, 4)
-    def _(k):
-        rows = rows_of(k, 16)
-        n = grads[0].shape[1] - HD
-        for h in range(2):
-            g = part(0, h, (rows, slice(0, HD)))
-            new(1, (rows, slice(h * HD, (h + 1) * HD)), g, matrix_rate, matrix_decay)
-            g = part(0, h, (rows, slice(HD, HD + n)))
-            new(3, (rows, slice(h * n, (h + 1) * n)), g, matrix_rate, matrix_decay)
-
-    done(1)
-    done(3)
-    for c in (*row_waits, *vec_waits):
+    for c in row_waits:
         c.wait()
     x_v, zero_v, one_v, dy_v = rows_in
 
@@ -1554,6 +1516,55 @@
 
     store(block_v, outs[0])
     store(grad_v, outs[1])
+    for c in waits[2]:
+        c.wait()
+
+    @pl.loop(0, 4)
+    def _(k):
+        rows = rows_of(k, 16)
+        for h in range(2):
+            n = grads[1].shape[1]
+            g = part(1, h, (rows, slice(0, n)))
+            new(2, (rows, slice(h * n, (h + 1) * n)), g, matrix_rate, matrix_decay)
+
+    done(2)
+    for c in waits[3]:
+        c.wait()
+
+    @pl.loop(0, 4)
+    def _(k):
+        rows = rows_of(k, 16)
+        n = grads[0].shape[1] - HD
+        for h in range(2):
+            g = part(0, h, (rows, slice(HD, HD + n)))
+            new(3, (rows, slice(h * n, (h + 1) * n)), g, matrix_rate, matrix_decay)
+
+    done(3)
+    for c in waits[0]:
+        c.wait()
+
+    @pl.loop(0, 4)
+    def _(k):
+        rows = rows_of(k, 16)
+        for c in range(3):
+            for h in range(2):
+                g = part(2, h, (rows, slice(c * HD, (c + 1) * HD)))
+                new(0, (c, rows, slice(h * HD, (h + 1) * HD)), g, matrix_rate, matrix_decay)
+
+    done(0)
+    for c in waits[1]:
+        c.wait()
+
+    @pl.loop(0, 4)
+    def _(k):
+        rows = rows_of(k, 16)
+        for h in range(2):
+            g = part(0, h, (rows, slice(0, HD)))
+            new(1, (rows, slice(h * HD, (h + 1) * HD)), g, matrix_rate, matrix_decay)
+
+    done(1)
+    for c in vec_waits:
+        c.wait()
     at = (slice(None), slice(None))
     shape = held[12].shape
     new(4, at, vec_sum[0 : shape[0], 0 : shape[1]], vector_rate, 0.0)

time: 175 us -> 176 us (level)
  no operation moved by 1% of the time
where the time goes in v2:
time: 176 us; the launch traced here: 175 us
  Pallas kernels  174 us (99%)
    pallas_call x1, Pallas kernels, forward(): pl.pallas_call(forward_kernel, out_shape=out, in_specs=[ANY, ANY, pl.Bloc...  83.9 us
    pallas_call x1, Pallas kernels, backward(): pl.pallas_call(backward_kernel, out_shape=out, in_specs=specs, out_specs=...  82.8 us
    pallas_call x1, Pallas kernels, update(): pl.pallas_call(update_kernel, out_shape=out, in_specs=specs, out_specs=[A...  7.85 us

profile of v2, /device:TPU:0, one launch (start us, length us, event | category | flops | bytes accessed | tf_op | source)
XLA Modules:
  0.0 175.3 jit_solution(3596757262701854496)
XLA Ops:
  0.7 83.9 %forward_and_gather.1 = (bf16[2,4,128,2048]{3,2,1,0:T(8,128)(2,1)}, bf16[4,4,2,64,1024]{4,3,2,1,0:T(8,128)(2,1)}, bf16[4,4,2,64,768]{4,3,2,1,0:T(8,128)(2,1)}, b...) custom-call(bf16[128,2048]{1,0:T(8,128)(2,1)} %refs_9_.1, ...), custom_call_target="tpu_custom_call" | custom-call | tf_op jit(solution)/shard_map/forward_and_gather/pallas_call | solution.py:784
  84.5 82.8 %backward_and_reduce.1 = (bf16[64,1280]{1,0:T(8,128)(2,1)}, bf16[64,1024]{1,0:T(8,128)(2,1)}, bf16[64,768]{1,0:T(8,128)(2,1)}, bf16[64,1280]{1,0:T(8,128)(2,1)},...) custom-call(bf16[2,2,2,128,2048]{4,3,2,1,0:T(8,128)(2,1)} %bitcast.1, ...), custom_call_target="tpu_custom_call" | custom-call | tf_op jit(solution)/shard_map/backward_and_reduce/pallas_call | solution.py:1429
  167.3 7.8 %update.1 = (bf16[128,2048]{1,0:T(8,128)(2,1)}, f32[128,2048]{1,0:T(8,128)}, f32[3,64,512]{2,1,0:T(8,128)}, f32[3,64,512]{2,1,0:T(8,128)}, f32[3,64,512]{2,1,0:T...) custom-call(bf16[64,1280]{1,0:T(8,128)(2,1)} %get-tuple-element.71.r, ...), custom_call_target="tpu_custom_call" | custom-call | tf_op jit(solution)/shard_map/update/pallas_call | solution.py:1589

commit v3 on v2

--- a/solution.py
+++ b/solution.py
@@ -143,19 +143,19 @@
 )
 BACKWARD_ORDER = (
     (FIRST, OD), (LOADS,), (CAT_GRADS, 0), (CAT_GRADS, 1), (CAT_GRADS, 2), (CAT_GRADS, 3),
-    (UP_GRADS, 0), (NEAR, OD, 1), (UP_GRADS, 1), (UP_GRADS, 2), (UP_GRADS, 3), (FIRST, UP),
-    (BRANCH, 0), (BRANCH, 1), (Z_MATE, 0), (BRANCH, 2), (BRANCH, 3), (Z_MATE, 1),
-    (ATTEND_BACK, 0), (Z_FIRST, 0), (NEAR, OD, 0), (ATTEND_BACK, 1), (QKV_GRADS, 0),
-    (Z_SECOND, 0), (QKV_GRADS, 1), (Z_FIRST, 1), (SECOND, OD, 1), (QKV_GRADS, 2), (QKV_GRADS, 3),
-    (FIRST, QKV), (NORM_GRADS, 0), (Z_MATE, 2), (Z_SECOND, 1), (FAR_SIDE, OD, 1), (NORM_GRADS, 1),
-    (Z_MATE, 3), (Z_FIRST, 2), (NEAR, UP, 0), (NEAR, UP, 1), (NORM_GRADS, 2), (Z_FIRST, 3),
-    (NEAR, QKV, 1), (Z_MATE, 4), (Z_SECOND, 2), (NORM_GRADS, 3), (Z_FINISH, 0), (FINISH, OD, 1),
-    (Z_FIRST, 4), (Z_MATE, 5), (SECOND, UP, 1), (VEC_ONE,), (SECOND, OD, 0), (Z_SECOND, 3),
-    (NEAR, QKV, 0), (SECOND, UP, 0), (Z_FIRST, 5), (Z_SECOND, 4), (FAR_SIDE, OD, 0),
-    (FAR_SIDE, UP, 1), (VEC_TWO,), (SECOND, QKV, 1), (Z_FINISH, 2), (Z_FINISH, 1), (VEC_THREE,),
-    (Z_SECOND, 5), (FAR_SIDE, UP, 0), (FINISH, UP, 1), (FAR_SIDE, QKV, 1), (SECOND, QKV, 0),
-    (FINISH, QKV, 1), (Z_FINISH, 3), (FINISH, UP, 0), (Z_FINISH, 4), (FINISH, OD, 0), (SETTLE,),
-    (FAR_SIDE, QKV, 0), (Z_FINISH, 5), (FINISH, QKV, 0),
+    (UP_GRADS, 0), (UP_GRADS, 1), (UP_GRADS, 2), (UP_GRADS, 3), (FIRST, UP), (BRANCH, 0),
+    (NEAR, OD, 0), (BRANCH, 1), (Z_MATE, 0), (NEAR, OD, 1), (BRANCH, 2), (BRANCH, 3),
+    (ATTEND_BACK, 0), (Z_MATE, 1), (Z_FIRST, 0), (ATTEND_BACK, 1), (QKV_GRADS, 0), (QKV_GRADS, 1),
+    (QKV_GRADS, 2), (Z_FIRST, 1), (Z_SECOND, 0), (QKV_GRADS, 3), (FIRST, QKV), (NEAR, UP, 0),
+    (NORM_GRADS, 0), (NORM_GRADS, 1), (Z_MATE, 3), (Z_MATE, 2), (Z_SECOND, 1), (NORM_GRADS, 2),
+    (Z_FINISH, 0), (Z_FIRST, 3), (NEAR, UP, 1), (NORM_GRADS, 3), (Z_FIRST, 2), (SECOND, OD, 1),
+    (Z_SECOND, 3), (Z_MATE, 5), (SECOND, UP, 0), (VEC_ONE,), (NEAR, QKV, 1), (FAR_SIDE, OD, 1),
+    (Z_SECOND, 2), (Z_MATE, 4), (Z_FIRST, 5), (SECOND, UP, 1), (FINISH, OD, 1), (NEAR, QKV, 0),
+    (Z_FIRST, 4), (Z_FINISH, 1), (FAR_SIDE, UP, 0), (Z_SECOND, 5), (VEC_TWO,), (SECOND, OD, 0),
+    (FAR_SIDE, UP, 1), (VEC_THREE,), (Z_FINISH, 3), (SECOND, QKV, 1), (Z_SECOND, 4),
+    (SECOND, QKV, 0), (FAR_SIDE, OD, 0), (FINISH, UP, 1), (FAR_SIDE, QKV, 1), (FAR_SIDE, QKV, 0),
+    (FINISH, QKV, 1), (Z_FINISH, 2), (FINISH, QKV, 0), (FINISH, OD, 0), (SETTLE,),
+    (FINISH, UP, 0), (Z_FINISH, 5), (Z_FINISH, 4),
 )
 
 
@@ -870,11 +870,15 @@
         return copy
 
     half_model = part_zero.shape[-1]
-    loads = [load(0, slope_in, dcat)]
+    loads = []
     for c in range(2):
         at = slice(c * half_model, (c + 1) * half_model)
-        loads.append(load(1 + c, dy_in.at[:, :, :, :, at], part_zero.at[c]))
-    od_loads = [load(13 + k, od_in.at[k], od_full.at[k]) for k in range(RING_SIZE)]
+        loads.append(load(c, dy_in.at[:, :, :, :, at], part_zero.at[c]))
+    thirds = (slice(0, 512), slice(512, 1024), slice(1024, 1280))
+    third_loads = []
+    for k, at in enumerate(thirds):
+        od_load = load(13 + k, od_in.at[:, :, :, :, at], od_full.at[:, :, :, :, at])
+        third_loads.append((od_load, load((2, 16, 17)[k], slope_in.at[:, at], dcat.at[:, at])))
     near_loads = []
     for way, half in enumerate((zl, other)):
         for d in range(2):
@@ -1121,12 +1125,12 @@
         return pltpu.make_async_copy(src, dst, out_sems.at[k])
 
     def cat_grads(hooks):
-        for c in od_loads:
-            c.wait()
-        thirds = (slice(0, 512), slice(512, 1024), slice(1024, 1280))
         for step, (m, at) in enumerate(((m, at) for at in thirds for m in range(2))):
             for entry in hooks.get(step, ()):
                 act(*entry)
+            if m == 0:
+                for c in third_loads[step // 2]:
+                    c.wait()
             w = od_full[:, :, :, :, at].reshape(-1, at.stop - at.start)
             rows = pl.ds(m * GROUP, GROUP)
             grad = nn(part_zero[0, m].reshape(GROUP, -1), w[:half_model])
@@ -1421,7 +1425,7 @@
         pltpu.SemaphoreType.DMA((6, 7)),
         pltpu.SemaphoreType.DMA((13,)),
         pltpu.SemaphoreType.DMA((13,)),
-        pltpu.SemaphoreType.DMA((17,)),
+        pltpu.SemaphoreType.DMA((18,)),
         pltpu.SemaphoreType.DMA((7, 2)),
         pltpu.SemaphoreType.DMA((9,)),
     ]

time: 176 us -> 175 us (level)
  no operation moved by 1% of the time
where the time goes in v3:
time: 175 us
  Pallas kernels  174 us (99%)
    pallas_call x1, Pallas kernels, forward(): pl.pallas_call(forward_kernel, out_shape=out, in_specs=[ANY, ANY, pl.Bloc...  83.9 us
    pallas_call x1, Pallas kernels, backward(): pl.pallas_call(backward_kernel, out_shape=out, in_specs=specs, out_specs=...  82 us
    pallas_call x1, Pallas kernels, update(): pl.pallas_call(update_kernel, out_shape=out, in_specs=specs, out_specs=[A...  7.85 us

profile of v3, /device:TPU:0, one launch (start us, length us, event | category | flops | bytes accessed | tf_op | source)
XLA Modules:
  0.0 174.6 jit_solution(2000159477893574886)
XLA Ops:
  0.7 83.9 %forward_and_gather.1 = (bf16[2,4,128,2048]{3,2,1,0:T(8,128)(2,1)}, bf16[4,4,2,64,1024]{4,3,2,1,0:T(8,128)(2,1)}, bf16[4,4,2,64,768]{4,3,2,1,0:T(8,128)(2,1)}, b...) custom-call(bf16[128,2048]{1,0:T(8,128)(2,1)} %refs_9_.1, ...), custom_call_target="tpu_custom_call" | custom-call | tf_op jit(solution)/shard_map/forward_and_gather/pallas_call | solution.py:784
  84.5 82.0 %backward_and_reduce.1 = (bf16[64,1280]{1,0:T(8,128)(2,1)}, bf16[64,1024]{1,0:T(8,128)(2,1)}, bf16[64,768]{1,0:T(8,128)(2,1)}, bf16[64,1280]{1,0:T(8,128)(2,1)},...) custom-call(bf16[2,2,2,128,2048]{4,3,2,1,0:T(8,128)(2,1)} %bitcast.1, ...), custom_call_target="tpu_custom_call" | custom-call | tf_op jit(solution)/shard_map/backward_and_reduce/pallas_call | solution.py:1433
  166.5 7.8 %update.1 = (bf16[128,2048]{1,0:T(8,128)(2,1)}, f32[128,2048]{1,0:T(8,128)}, f32[3,64,512]{2,1,0:T(8,128)}, f32[3,64,512]{2,1,0:T(8,128)}, f32[3,64,512]{2,1,0:T...) custom-call(bf16[64,1280]{1,0:T(8,128)(2,1)} %get-tuple-element.71.r, ...), custom_call_target="tpu_custom_call" | custom-call | tf_op jit(solution)/shard_map/update/pallas_call | solution.py:1593
